TPU v7x, 512 devices: a whole 4x4x16 slice. The times are simulated.
512 devices in a mesh: seq: 64 (over x, z_lo, core), head: 8 (over y, z_hi).
Axes of the slice: x: 4, y: 4, z: 16 (z_hi: 2, z_lo: 8; z = z_hi * 8 + z_lo), core: 2. Of those that a mesh axis runs over, the one named last changes fastest.
Arguments:
- q_lat: bfloat16 [8192, 64, 512], P('seq', 'head'), may hold values from -6 to 6
- q_rope: bfloat16 [8192, 4096], P('seq', 'head'), may hold values from -6 to 6
- d_out: bfloat16 [8192, 64, 512], P('seq', 'head'), may hold values from -12 to 12
- latent: bfloat16 [8192, 512], P('seq'), may hold values from -6 to 6
- key_rope: bfloat16 [64, 8192], P(None, 'seq'), may hold values from -6 to 6
- forward_dot: float32 [64, 8192], P('head', 'seq'), may hold values from -120 to 120
- log_total: float32 [64, 8192], P('head', 'seq'), may hold values from 6 to 9
- block_order: int32 [128], replicated, may hold values from 0 to 127, as said below
Outputs:
- grad_q_lat: bfloat16 [8192, 64, 512], P('seq', 'head')
- grad_q_rope: bfloat16 [8192, 4096], P('seq', 'head')
- grad_latent: bfloat16 [8192, 512], P(('seq', 'head'))
- grad_key_rope: bfloat16 [8192, 64], P(('seq', 'head'))
Inputs may be any that keep to these rules, and one draw needn't show every extreme that they name: `block_order`: each seq index's two entries are a and 127 - a in either order, and over the 64 indices the values a run through 0 to 63 once each.
All inputs are finite; a program needn't handle non-finite values.
Results may differ from a plain program's by a relative error of at most 0.008.
Values may be sent and summed in bfloat16 or wider, within the bound.
No kernel may reach another device: no remote copies, remote signals or barrier semaphores. Data moves between devices by JAX's collectives and lax.ppermute only.
A program may use at most 64 MiB of HBM per device.

v0:
```python
import jax
import jax.numpy as jnp
from jax import lax
from jax.sharding import PartitionSpec as P

SPAN = 4


SOFTMAX_SCALE = 192.0 ** (-0.5)
MASKED = -1e30


def from_behind(value, axis, by):
    devices = lax.axis_size(axis)
    return lax.ppermute(value, axis, [(i, (i + by) % devices) for i in range(devices)])


def score_tile(key_rows, rope_keys, q_rows, rope_rows):
    lat_part = jnp.einsum("kd,rd->kr", key_rows, q_rows, preferred_element_type=jnp.float32)
    rope_part = jnp.einsum("ek,re->kr", rope_keys, rope_rows, preferred_element_type=jnp.float32)
    return SOFTMAX_SCALE * (lat_part + rope_part)


def grad_tile(key_rows, rope_keys, q_rows, rope_rows, grad_rows, total_rows, dot_rows, visible):
    scores = score_tile(key_rows, rope_keys, q_rows, rope_rows)
    shifted = scores - total_rows[None, :]
    if visible is not None:
        shifted = jnp.where(visible, shifted, MASKED)
    probs = jnp.exp(shifted)
    dprobs = jnp.einsum("kd,rd->kr", key_rows, grad_rows, preferred_element_type=jnp.float32)
    dscores = (SOFTMAX_SCALE * probs * (dprobs - dot_rows[None, :])).astype(jnp.bfloat16)
    probs_low = probs.astype(jnp.bfloat16)
    grad_query = jnp.einsum("kr,kd->rd", dscores, key_rows, preferred_element_type=jnp.float32)
    grad_rope = jnp.einsum("kr,ek->re", dscores, rope_keys, preferred_element_type=jnp.float32)
    latent_part = jnp.einsum(
        "kr,rd->kd", dscores, q_rows, preferred_element_type=jnp.float32
    ) + jnp.einsum("kr,rd->kd", probs_low, grad_rows, preferred_element_type=jnp.float32)
    keyrope_part = jnp.einsum("kr,re->ke", dscores, rope_rows, preferred_element_type=jnp.float32)
    return (grad_query, grad_rope, latent_part, keyrope_part)


def lower_slot(vis_blocks):
    return jnp.where(vis_blocks[0] < vis_blocks[1], 0, 1)


def pass_keys(vis_keys):
    return from_behind((vis_keys[0], vis_keys[1]), "seq", 1)


def head_share(lat_part, rope_part):
    return (lat_part, rope_part)


def shards(q_lat, q_rope, d_out, latent, key_rope, forward_dot, log_total, block_order):
    tok_rows, head_count, lat_width = q_lat.shape
    rope_width = key_rope.shape[0]
    blk_len = tok_rows // 2
    row_count = tok_rows * head_count
    blk_rows = blk_len * head_count
    window_len = SPAN
    queries = q_lat.reshape(row_count, lat_width)
    rope_queries = q_rope.reshape(row_count, rope_width)
    out_grads = d_out.reshape(row_count, lat_width)
    row_dots = forward_dot.T.reshape(row_count)
    row_totals = log_total.T.reshape(row_count)
    cycle_len = lax.axis_size("seq")
    my_index = lax.axis_index("seq")
    block_pairs = block_order.reshape(cycle_len, 2)
    own_blocks = lax.dynamic_index_in_dim(block_pairs, my_index, 0, keepdims=False)
    low_mine = jnp.minimum(own_blocks[0], own_blocks[1])
    high_slot = jnp.where(own_blocks[0] > own_blocks[1], 0, 1)
    token_ids = jnp.arange(tok_rows, dtype=jnp.int32)
    key_positions = (
        jnp.where(token_ids < blk_len, own_blocks[0], own_blocks[1]) * blk_len + token_ids % blk_len
    )
    row_positions = jnp.repeat(key_positions, head_count)
    visible = key_positions[:, None] <= row_positions[None, :]
    grad_q, grad_qr, own_lat, own_rope = grad_tile(
        latent, key_rope, queries, rope_queries, out_grads, row_totals, row_dots, visible
    )
    totals = head_share(own_lat, own_rope)
    vis_keys = (latent, key_rope)
    for step_idx in range(1, window_len):
        vis_keys = pass_keys(vis_keys)
        totals = from_behind((totals[0], totals[1]), "seq", 1)
        vis_lat = vis_keys[0]
        vis_rope = vis_keys[1]
        vis_blocks = lax.dynamic_index_in_dim(
            block_pairs, (my_index - step_idx) % cycle_len, 0, keepdims=False
        )
        low_vis = jnp.minimum(vis_blocks[0], vis_blocks[1])

        def whole_rows():
            begin = lower_slot(vis_blocks) * blk_len
            key_rows = lax.dynamic_slice_in_dim(vis_lat, begin, blk_len, 0)
            rope_keys = lax.dynamic_slice_in_dim(vis_rope, begin, blk_len, 1)
            query_part, qrope_part, latent_part, keyrope_part = grad_tile(
                key_rows, rope_keys, queries, rope_queries, out_grads, row_totals, row_dots, None
            )
            latent_full = lax.dynamic_update_slice_in_dim(
                jnp.zeros((tok_rows, lat_width), jnp.float32), latent_part, begin, 0
            )
            keyrope_full = lax.dynamic_update_slice_in_dim(
                jnp.zeros((tok_rows, rope_width), jnp.float32), keyrope_part, begin, 0
            )
            return (grad_q + query_part, grad_qr + qrope_part, latent_full, keyrope_full)

        def upper_rows():
            begin = high_slot * blk_rows
            query_part, qrope_part, latent_part, keyrope_part = grad_tile(
                vis_lat,
                vis_rope,
                lax.dynamic_slice_in_dim(queries, begin, blk_rows, 0),
                lax.dynamic_slice_in_dim(rope_queries, begin, blk_rows, 0),
                lax.dynamic_slice_in_dim(out_grads, begin, blk_rows, 0),
                lax.dynamic_slice_in_dim(row_totals, begin, blk_rows, 0),
                lax.dynamic_slice_in_dim(row_dots, begin, blk_rows, 0),
                None,
            )
            new_q = lax.dynamic_update_slice_in_dim(
                grad_q, lax.dynamic_slice_in_dim(grad_q, begin, blk_rows, 0) + query_part, begin, 0
            )
            new_qr = lax.dynamic_update_slice_in_dim(
                grad_qr,
                lax.dynamic_slice_in_dim(grad_qr, begin, blk_rows, 0) + qrope_part,
                begin,
                0,
            )
            return (new_q, new_qr, latent_part, keyrope_part)

        grad_q, grad_qr, lat_part, rope_part = lax.cond(low_mine > low_vis, whole_rows, upper_rows)
        new_part = head_share(lat_part, rope_part)
        totals = (totals[0] + new_part[0], totals[1] + new_part[1])
    totals = from_behind((totals[0], totals[1]), "seq", 1 - window_len)
    totals = (
        lax.psum_scatter(totals[0], "head", scatter_dimension=0, tiled=True),
        lax.psum_scatter(totals[1], "head", scatter_dimension=0, tiled=True),
    )
    return (
        grad_q.astype(jnp.bfloat16).reshape(tok_rows, head_count, lat_width),
        grad_qr.astype(jnp.bfloat16).reshape(tok_rows, head_count * rope_width),
        totals[0].astype(jnp.bfloat16),
        totals[1].astype(jnp.bfloat16),
    )


def solution(mesh):
    return jax.shard_map(
        shards,
        mesh=mesh,
        in_specs=(
            P("seq", "head", None),
            P("seq", "head"),
            P("seq", "head", None),
            P("seq", None),
            P(None, "seq"),
            P("head", "seq"),
            P("head", "seq"),
            P(),
        ),
        out_specs=(
            P("seq", "head", None),
            P("seq", "head"),
            P(("seq", "head"), None),
            P(("seq", "head"), None),
        ),
        check_vma=False,
    )
```

profile of v0, /device:TPU:1, one launch (start us, length us, event | category | flops | bytes accessed | tf_op | source)
XLA Modules:
  0.0 384.3 jit_solution(6357352953947671225)
XLA Ops:
  7.2 5.1 %collective-permute-start.3 = (bf16[64,128]{1,0:T(8,128)(2,1)}, bf16[64,128]{1,0:T(8,128)(2,1)S(1)}, u32[]{:S(2)}, u32[]{:S(2)}) collective-permute-start(bf16[64,128]{1,0:T(8,128)(2,1)} %param.18), channel_id=1, source_target_pairs={{0,8},{8,16},{16,24},{24,32},{32,40},{40,48},{48,56},{56,64},{64,7... | collective-permute-start | bytes 49160 | tf_op jit(solution)/shard_map/ppermute | solution.py:15
  12.3 1.9 collective-permute-start
  21.1 1.4 fusion.128
  24.4 3.9 %collective-permute-start.6 = (f32[128,512]{1,0:T(8,128)}, f32[128,512]{1,0:T(8,128)}, u32[]{:S(2)}, u32[]{:S(2)}) collective-permute-start(f32[128,512]{1,0:T(8,128)} %convolution_add_fusion.24), channel_id=1, source_target_pairs={{0,8},{8,16},{16,24},{24,32},{32,40},{40,48},{48,56},{56,64},{64,7... | collective-permute-start | bytes 786440 | tf_op jit(solution)/shard_map/ppermute | solution.py:15
  28.3 1.8 fusion.153
  34.9 5.7 %conditional.3 = (f32[1024,512]{1,0:T(8,128)}, f32[1024,64]{0,1:T(8,128)S(1)}, f32[128,512]{1,0:T(8,128)}, f32[128,64]{0,1:T(8,128)}) conditional(s32[]{:T(128)} %convert_element_type.73, (s32[]{:T(128)}, f32[1024,512]{1,0:T(8,128)}, bf16[1024,512]{1,0:T(8,128)(2,1)S(1)}, bf16[128,512]{1,0:T(8,128)(2,1)S(1)}, bf16[1024,64]{1,0:T(8,128)(2,1)S(1)}, ...), branch_computations={%region_0.1_spmd, %region_1.2_spmd} | conditional | flops 361857024 | bytes 12148916 | solution.py:131
  36.7 2.5 fusion
  40.6 1.8 add.208
  42.3 8.7 %collective-permute-start.7 = (f32[128,512]{1,0:T(8,128)}, f32[128,512]{1,0:T(8,128)}, u32[]{:S(2)}, u32[]{:S(2)}) collective-permute-start(f32[128,512]{1,0:T(8,128)} %add.208), channel_id=1, source_target_pairs={{0,8},{8,16},{16,24},{24,32},{32,40},{40,48},{48,56},{56,64},{64,7... | collective-permute-start | bytes 786440 | tf_op jit(solution)/shard_map/ppermute | solution.py:15
  51.0 1.9 collective-permute-start.1
  53.0 3.9 %collective-permute-start.4 = (bf16[64,128]{1,0:T(8,128)(2,1)S(1)}, bf16[64,128]{1,0:T(8,128)(2,1)}, u32[]{:S(2)}, u32[]{:S(2)}) collective-permute-start(bf16[64,128]{1,0:T(8,128)(2,1)S(1)} %collective-permute-done.3), channel_id=1, source_target_pairs={{0,8},{8,16},{16,24},{24,32},{32,40},{40,48},{48,56},{56,64},{64,7... | collective-permute-start | bytes 49160 | tf_op jit(solution)/shard_map/ppermute | solution.py:15
  58.2 8.5 %conditional.4 = (f32[1024,512]{1,0:T(8,128)}, f32[1024,64]{0,1:T(8,128)S(1)}, f32[128,512]{1,0:T(8,128)}, f32[128,64]{0,1:T(8,128)}) conditional(s32[]{:T(128)} %convert_element_type.72, (s32[]{:T(128)}, f32[1024,512]{1,0:T(8,128)}, bf16[1024,512]{1,0:T(8,128)(2,1)S(1)}, bf16[128,512]{1,0:T(8,128)(2,1)S(1)}, bf16[1024,64]{1,0:T(8,128)(2,1)S(1)}, ...), branch_computations={%region_2.3_spmd, %region_3.4_spmd} | conditional | flops 361857024 | bytes 12132504 | solution.py:131
  62.1 2.5 fusion.41
  66.7 1.8 add.209
  68.5 3.8 %collective-permute-start.8 = (f32[128,512]{1,0:T(8,128)}, f32[128,512]{1,0:T(8,128)}, u32[]{:S(2)}, u32[]{:S(2)}) collective-permute-start(f32[128,512]{1,0:T(8,128)} %add.209), channel_id=1, source_target_pairs={{0,8},{8,16},{16,24},{24,32},{32,40},{40,48},{48,56},{56,64},{64,7... | collective-permute-start | bytes 786440 | tf_op jit(solution)/shard_map/ppermute | solution.py:15
  72.3 3.1 collective-permute-start.2
  75.4 3.9 %collective-permute-start.5 = (bf16[64,128]{1,0:T(8,128)(2,1)}, bf16[64,128]{1,0:T(8,128)(2,1)S(1)}, u32[]{:S(2)}, u32[]{:S(2)}) collective-permute-start(bf16[64,128]{1,0:T(8,128)(2,1)} %collective-permute-done.4), channel_id=1, source_target_pairs={{0,8},{8,16},{16,24},{24,32},{32,40},{40,48},{48,56},{56,64},{64,7... | collective-permute-start | bytes 49160 | tf_op jit(solution)/shard_map/ppermute | solution.py:15
  80.5 11.0 %collective-permute-done.5 = bf16[64,128]{1,0:T(8,128)(2,1)S(1)} collective-permute-done((bf16[64,128]{1,0:T(8,128)(2,1)}, bf16[64,128]{1,0:T(8,128)(2,1)S(1)}, u32[]{:S(2)}, u32[]{:S(2)}) %collective-permute-start.5) | collective-permute-done | bytes 16416 | tf_op jit(solution)/shard_map/ppermute | solution.py:15
  91.5 10.2 %conditional.5 = (f32[128,512]{1,0:T(8,128)}, f32[128,64]{0,1:T(8,128)S(1)}, bf16[128,8,512]{2,1,0:T(8,128)(2,1)}, bf16[128,512]{1,0:T(8,128)(2,1)}) conditional(s32[]{:T(128)} %convert_element_type.71, (s32[]{:T(128)}, bf16[1024,512]{1,0:T(8,128)(2,1)S(1)}, bf16[128,512]{1,0:T(8,128)(2,1)S(1)}, bf16[1024,64]{1,0:T(8,128)(2,1)S(1)}, ...), branch_computations={%region_4.5_spmd, %region_5.6_spmd} | conditional | flops 362446848 | bytes 12005494 | solution.py:131
  94.0 2.5 fusion.82
  96.5 2.7 convert_bitcast_fusion
  102.7 14.8 %collective-permute-start.9 = (f32[128,512]{1,0:T(8,128)S(1)}, f32[128,512]{1,0:T(8,128)S(1)}, u32[]{:S(2)}, u32[]{:S(2)}) collective-permute-start(f32[128,512]{1,0:T(8,128)S(1)} %add.210), channel_id=1, source_target_pairs={{0,488},{8,496},{16,504},{24,0},{32,8},{40,16},{48,24},{56,32},{64... | collective-permute-start | bytes 786440 | tf_op jit(solution)/shard_map/ppermute | solution.py:15
  117.8 1.9 collective-permute-start.10
  119.7 4.3 %collective-permute-done.10 = f32[128,64]{0,1:T(8,128)S(1)} collective-permute-done((f32[128,64]{0,1:T(8,128)S(1)}, f32[128,64]{0,1:T(8,128)S(1)}, u32[]{:S(2)}, u32[]{:S(2)}) %collective-permute-start.10) | collective-permute-done | bytes 32800 | tf_op jit(solution)/shard_map/ppermute | solution.py:15
  124.8 4.4 %collective-permute-start.11 = (f32[128,64]{0,1:T(8,128)S(1)}, f32[128,64]{0,1:T(8,128)S(1)}, u32[]{:S(2)}, u32[]{:S(2)}) collective-permute-start(f32[128,64]{0,1:T(8,128)S(1)} %add.211), channel_id=1, source_target_pairs={{0,8},{8,16},{16,24},{24,32},{32,40},{40,48},{48,56},{56,64},{64,7... | collective-permute-start | bytes 98312 | tf_op jit(solution)/shard_map/ppermute | solution.py:15
  129.2 5.8 %collective-permute-done.11 = f32[128,64]{0,1:T(8,128)S(1)} collective-permute-done((f32[128,64]{0,1:T(8,128)S(1)}, f32[128,64]{0,1:T(8,128)S(1)}, u32[]{:S(2)}, u32[]{:S(2)}) %collective-permute-start.11) | collective-permute-done | bytes 32800 | tf_op jit(solution)/shard_map/ppermute | solution.py:15
  135.8 1.9 collective-permute-start.12
  137.7 12.0 %collective-permute-done.12 = f32[128,64]{0,1:T(8,128)S(1)} collective-permute-done((f32[128,64]{0,1:T(8,128)S(1)}, f32[128,64]{0,1:T(8,128)S(1)}, u32[]{:S(2)}, u32[]{:S(2)}) %collective-permute-start.12) | collective-permute-done | bytes 32800 | tf_op jit(solution)/shard_map/ppermute | solution.py:15
  149.7 1.9 collective-permute-start.13
  151.6 4.2 %collective-permute-done.13 = f32[128,64]{0,1:T(8,128)S(1)} collective-permute-done((f32[128,64]{0,1:T(8,128)S(1)}, f32[128,64]{0,1:T(8,128)S(1)}, u32[]{:S(2)}, u32[]{:S(2)}) %collective-permute-start.13) | collective-permute-done | bytes 32800 | tf_op jit(solution)/shard_map/ppermute | solution.py:15
  157.4 113.7 %reduce-scatter.7.cloned.1.call-done = f32[16,64]{1,0:T(8,128)} async-done(((f32[128,64]{1,0:T(8,128)}), f32[16,64]{1,0:T(8,128)}) %reduce-scatter.7.cloned.1.call-update) | async-done | bytes 4112
  272.6 103.6 %reduce-scatter.5.cloned.1.call-done = f32[16,512]{1,0:T(8,128)} async-done(((f32[128,512]{1,0:T(8,128)}), f32[16,512]{1,0:T(8,128)}) %reduce-scatter.5.cloned.1.call-update) | async-done | bytes 32784 | tf_op jit(solution)/shard_map/reduce_scatter | solution.py:136
  (87 shorter events, 30.7 us)
Async XLA Ops:
  7.2 15.4 %copy-start.2 = (bf16[128,512]{1,0:T(8,128)(2,1)S(1)}, bf16[128,512]{1,0:T(8,128)(2,1)}, u32[]{:S(2)}) copy-start(bf16[128,512]{1,0:T(8,128)(2,1)} %param.17) | copy-start | bytes 393220
  7.2 13.9 %copy-start = (bf16[128,8,512]{2,1,0:T(8,128)(2,1)S(1)}, bf16[128,8,512]{2,1,0:T(8,128)(2,1)}, u32[]{:S(2)}) copy-start(bf16[128,8,512]{2,1,0:T(8,128)(2,1)} %param.14) | copy-start | bytes 3145732
  7.2 15.4 %copy-start.1 = (bf16[128,8,512]{2,1,0:T(8,128)(2,1)S(1)}, bf16[128,8,512]{2,1,0:T(8,128)(2,1)}, u32[]{:S(2)}) copy-start(bf16[128,8,512]{2,1,0:T(8,128)(2,1)} %param.16) | copy-start | bytes 3145732
  7.2 263.9 %reduce-scatter.7.cloned.1.call-start = ((), (), s32[]{:S(2)}) async-start(), calls=%async_computation.3 | async-start | bytes 73728
  7.2 27.6 %collective-permute-start.3 = (bf16[64,128]{1,0:T(8,128)(2,1)}, bf16[64,128]{1,0:T(8,128)(2,1)S(1)}, u32[]{:S(2)}, u32[]{:S(2)}) collective-permute-start(bf16[64,128]{1,0:T(8,128)(2,1)} %param.18), channel_id=1, source_target_pairs={{0,8},{8,16},{16,24},{24,32},{32,40},{40,48},{48,56},{56,64},{64,7... | collective-permute-start | bytes 49160 | tf_op jit(solution)/shard_map/ppermute | solution.py:15
  12.3 22.5 %collective-permute-start = (bf16[128,512]{1,0:T(8,128)(2,1)}, bf16[128,512]{1,0:T(8,128)(2,1)S(1)}, u32[]{:S(2)}, u32[]{:S(2)}) collective-permute-start(bf16[128,512]{1,0:T(8,128)(2,1)} %param.17), channel_id=1, source_target_pairs={{0,8},{8,16},{16,24},{24,32},{32,40},{40,48},{48,56},{56,64},{64,7... | collective-permute-start | bytes 393224 | tf_op jit(solution)/shard_map/ppermute | solution.py:15
  15.2 0.6 copy-start.10
  15.2 15.2 %copy-start.11 = (s32[1,2]{1,0:T(1,128)}, s32[1,2]{1,0:T(1,128)S(1)}, u32[]{:S(2)}) copy-start(s32[1,2]{1,0:T(1,128)S(1)} %get-tuple-element.232) | copy-start | bytes 28
  18.1 16.7 %copy-start.7 = (f32[1024]{0:T(1024)}, f32[1024]{0:T(1024)S(1)}, u32[]{:S(2)}) copy-start(f32[1024]{0:T(1024)S(1)} %reshape.123) | copy-start | bytes 12292
  19.0 15.9 %copy-start.8 = (f32[1024]{0:T(1024)}, f32[1024]{0:T(1024)S(1)}, u32[]{:S(2)}) copy-start(f32[1024]{0:T(1024)S(1)} %reshape.121) | copy-start | bytes 12292
  23.3 6.8 %copy-start.6 = (bf16[64,128]{1,0:T(8,128)(2,1)S(1)}, bf16[64,128]{1,0:T(8,128)(2,1)}, u32[]{:S(2)}) copy-start(bf16[64,128]{1,0:T(8,128)(2,1)} %param.18) | copy-start | bytes 49156
  24.4 16.2 %collective-permute-start.6 = (f32[128,512]{1,0:T(8,128)}, f32[128,512]{1,0:T(8,128)}, u32[]{:S(2)}, u32[]{:S(2)}) collective-permute-start(f32[128,512]{1,0:T(8,128)} %convolution_add_fusion.24), channel_id=1, source_target_pairs={{0,8},{8,16},{16,24},{24,32},{32,40},{40,48},{48,56},{56,64},{64,7... | collective-permute-start | bytes 786440 | tf_op jit(solution)/shard_map/ppermute | solution.py:15
  42.3 24.3 %collective-permute-start.7 = (f32[128,512]{1,0:T(8,128)}, f32[128,512]{1,0:T(8,128)}, u32[]{:S(2)}, u32[]{:S(2)}) collective-permute-start(f32[128,512]{1,0:T(8,128)} %add.208), channel_id=1, source_target_pairs={{0,8},{8,16},{16,24},{24,32},{32,40},{40,48},{48,56},{56,64},{64,7... | collective-permute-start | bytes 786440 | tf_op jit(solution)/shard_map/ppermute | solution.py:15
  51.0 7.1 %collective-permute-start.1 = (bf16[128,512]{1,0:T(8,128)(2,1)S(1)}, bf16[128,512]{1,0:T(8,128)(2,1)S(1)}, u32[]{:S(2)}, u32[]{:S(2)}) collective-permute-start(bf16[128,512]{1,0:T(8,128)(2,1)S(1)} %collective-permute-done), channel_id=1, source_target_pairs={{0,8},{8,16},{16,24},{24,32},{32,40},{40,48},{48,56},{56,64},{64,7... | collective-permute-start | bytes 393224 | tf_op jit(solution)/shard_map/ppermute | solution.py:15
  53.0 5.2 %collective-permute-start.4 = (bf16[64,128]{1,0:T(8,128)(2,1)S(1)}, bf16[64,128]{1,0:T(8,128)(2,1)}, u32[]{:S(2)}, u32[]{:S(2)}) collective-permute-start(bf16[64,128]{1,0:T(8,128)(2,1)S(1)} %collective-permute-done.3), channel_id=1, source_target_pairs={{0,8},{8,16},{16,24},{24,32},{32,40},{40,48},{48,56},{56,64},{64,7... | collective-permute-start | bytes 49160 | tf_op jit(solution)/shard_map/ppermute | solution.py:15
  68.5 33.2 %collective-permute-start.8 = (f32[128,512]{1,0:T(8,128)}, f32[128,512]{1,0:T(8,128)}, u32[]{:S(2)}, u32[]{:S(2)}) collective-permute-start(f32[128,512]{1,0:T(8,128)} %add.209), channel_id=1, source_target_pairs={{0,8},{8,16},{16,24},{24,32},{32,40},{40,48},{48,56},{56,64},{64,7... | collective-permute-start | bytes 786440 | tf_op jit(solution)/shard_map/ppermute | solution.py:15
  72.3 19.2 %collective-permute-start.2 = (bf16[128,512]{1,0:T(8,128)(2,1)S(1)}, bf16[128,512]{1,0:T(8,128)(2,1)S(1)}, u32[]{:S(2)}, u32[]{:S(2)}) collective-permute-start(bf16[128,512]{1,0:T(8,128)(2,1)S(1)} %collective-permute-done.1), channel_id=1, source_target_pairs={{0,8},{8,16},{16,24},{24,32},{32,40},{40,48},{48,56},{56,64},{64,7... | collective-permute-start | bytes 393224 | tf_op jit(solution)/shard_map/ppermute | solution.py:15
  75.4 16.0 %collective-permute-start.5 = (bf16[64,128]{1,0:T(8,128)(2,1)}, bf16[64,128]{1,0:T(8,128)(2,1)S(1)}, u32[]{:S(2)}, u32[]{:S(2)}) collective-permute-start(bf16[64,128]{1,0:T(8,128)(2,1)} %collective-permute-done.4), channel_id=1, source_target_pairs={{0,8},{8,16},{16,24},{24,32},{32,40},{40,48},{48,56},{56,64},{64,7... | collective-permute-start | bytes 49160 | tf_op jit(solution)/shard_map/ppermute | solution.py:15
  102.7 53.9 %collective-permute-start.9 = (f32[128,512]{1,0:T(8,128)S(1)}, f32[128,512]{1,0:T(8,128)S(1)}, u32[]{:S(2)}, u32[]{:S(2)}) collective-permute-start(f32[128,512]{1,0:T(8,128)S(1)} %add.210), channel_id=1, source_target_pairs={{0,488},{8,496},{16,504},{24,0},{32,8},{40,16},{48,24},{56,32},{64... | collective-permute-start | bytes 786440 | tf_op jit(solution)/shard_map/ppermute | solution.py:15
  117.8 6.2 %collective-permute-start.10 = (f32[128,64]{0,1:T(8,128)S(1)}, f32[128,64]{0,1:T(8,128)S(1)}, u32[]{:S(2)}, u32[]{:S(2)}) collective-permute-start(f32[128,64]{0,1:T(8,128)S(1)} %fusion.154), channel_id=1, source_target_pairs={{0,8},{8,16},{16,24},{24,32},{32,40},{40,48},{48,56},{56,64},{64,7... | collective-permute-start | bytes 98312 | tf_op jit(solution)/shard_map/ppermute | solution.py:15
  124.8 10.2 %collective-permute-start.11 = (f32[128,64]{0,1:T(8,128)S(1)}, f32[128,64]{0,1:T(8,128)S(1)}, u32[]{:S(2)}, u32[]{:S(2)}) collective-permute-start(f32[128,64]{0,1:T(8,128)S(1)} %add.211), channel_id=1, source_target_pairs={{0,8},{8,16},{16,24},{24,32},{32,40},{40,48},{48,56},{56,64},{64,7... | collective-permute-start | bytes 98312 | tf_op jit(solution)/shard_map/ppermute | solution.py:15
  135.8 14.0 %collective-permute-start.12 = (f32[128,64]{0,1:T(8,128)S(1)}, f32[128,64]{0,1:T(8,128)S(1)}, u32[]{:S(2)}, u32[]{:S(2)}) collective-permute-start(f32[128,64]{0,1:T(8,128)S(1)} %add.212), channel_id=1, source_target_pairs={{0,8},{8,16},{16,24},{24,32},{32,40},{40,48},{48,56},{56,64},{64,7... | collective-permute-start | bytes 98312 | tf_op jit(solution)/shard_map/ppermute | solution.py:15
  149.7 6.1 %collective-permute-start.13 = (f32[128,64]{0,1:T(8,128)S(1)}, f32[128,64]{0,1:T(8,128)S(1)}, u32[]{:S(2)}, u32[]{:S(2)}) collective-permute-start(f32[128,64]{0,1:T(8,128)S(1)} %add.213), channel_id=1, source_target_pairs={{0,488},{8,496},{16,504},{24,0},{32,8},{40,16},{48,24},{56,32},{64... | collective-permute-start | bytes 98312 | tf_op jit(solution)/shard_map/ppermute | solution.py:15
  156.6 219.5 %reduce-scatter.5.cloned.1.call-start = ((), (), s32[]{:S(2)}) async-start(), calls=%async_computation.2 | async-start | bytes 294912 | tf_op jit(solution)/shard_map/reduce_scatter | solution.py:136
  156.7 0.7 copy-start.3
Sparse Core Ops, SparseCore 0:
  156.7 114.3 reduce-scatter.6
  275.5 100.5 reduce-scatter.4
where the time goes:
time: 384 us
  waiting for transfers between devices  255 us (66%)
  starting transfers between devices  61.3 us (16%)
  matrix products  23.7 us (6%)
  between operations  20.8 us (5%)
  local copies, waits for them, and re-layouts  12.3 us (3%)
  other arithmetic  11.5 us (3%)
    unnamed x3, waiting for transfers between devices  114 us
    reduce_scatter x1, waiting for transfers between devices, shards(): lax.psum_scatter(totals[0], 'head', scatter_dimension=0, tiled=True)  104 us
    ppermute x14, starting transfers between devices, from_behind(): lax.ppermute(value, axis, [(i, (i + by) % devices) for i in range(devices)])  61.2 us
    ppermute x14, waiting for transfers between devices, from_behind(): lax.ppermute(value, axis, [(i, (i + by) % devices) for i in range(devices)])  37.4 us
    dot_general x4, matrix products, grad_tile(): jnp.einsum('kr,kd->rd', dscores, key_rows, preferred_element_type=jnp.flo...  9.28 us
  transfers between devices with their start and end apart: 16, of which 7 were waited for; matrix products, arithmetic and copies ran while one was open for 11% of the time, Pallas kernels for 0%

commit v1 on v0

v1 whole, which is shorter than its diff:
```python
import jax
import jax.numpy as jnp
from jax import lax
from jax.experimental import pallas as pl
from jax.experimental.pallas import tpu as pltpu
from jax.sharding import PartitionSpec as P

SPAN = 4
SOFTMAX_SCALE = 192.0 ** (-0.5)
BLK = 64
RUN = 16
ORDER = (0, 2, 1, 3)


def shift(value, by):
    seqs, heads = lax.axis_size("seq"), lax.axis_size("head")
    pairs = []
    for i in range(seqs):
        j = (i + by) % seqs
        for h in range(heads):
            pairs.append((i * heads + h, j * heads + (h ^ 1 if i // RUN != j // RUN else h)))
    return lax.ppermute(value, ("seq", "head"), pairs)


def nt(a, b):
    return lax.dot_general(a, b, (((1,), (1,)), ((), ())), preferred_element_type=jnp.float32)


def nn(a, b):
    return lax.dot_general(a, b, (((1,), (0,)), ((), ())), preferred_element_type=jnp.float32)


def tn(a, b):
    return lax.dot_general(a, b, (((0,), (0,)), ((), ())), preferred_element_type=jnp.float32)


def rope_of(packed):
    wide = jnp.concatenate([packed[:, 128 * b : 128 * (b + 1)] for b in range(4)], axis=0)
    return wide.astype(jnp.float32).T.astype(jnp.bfloat16)


def attention_kernel(
    index_ref, order_ref, own_ref, ka_ref, kb_ref, kc_ref, q_ref, qr_ref, do_ref, dot_ref, tot_ref,
    gq_ref, gqr_ref, send_ref, keep_ref,
    rope_ref,
):
    me = index_ref[0]
    seqs = order_ref.shape[0] // 2
    shard_refs = {0: own_ref, 2: ka_ref, 1: kb_ref, 3: kc_ref}
    rows = q_ref.shape[0] // 2
    heads = rows // BLK
    own_first, own_second = order_ref[2 * me], order_ref[2 * me + 1]
    high = jnp.where(own_first > own_second, 0, 1)
    low_mine = jnp.minimum(own_first, own_second)
    high_mine = jnp.maximum(own_first, own_second)
    upper = pl.ds(pl.multiple_of(high * rows, rows), rows)
    lower = pl.ds(pl.multiple_of((1 - high) * rows, rows), rows)

    low_keys, high_keys, low_ropes, high_ropes = [], [], [], []
    low_blocks, high_blocks, low_at, high_at = [], [], [], []
    for place, s in enumerate(ORDER):
        ref = shard_refs[s]
        other = lax.rem(me + seqs - s, seqs)
        first, second = order_ref[2 * other], order_ref[2 * other + 1]
        low_slot = jnp.where(first < second, 0, 1)
        at_low = pl.multiple_of(low_slot * BLK, BLK)
        at_high = pl.multiple_of((1 - low_slot) * BLK, BLK)
        rope_ref[place] = rope_of(ref[2 * BLK :, :])
        low_keys.append(ref[pl.ds(at_low, BLK), :])
        high_keys.append(ref[pl.ds(at_high, BLK), :])
        low_ropes.append(rope_ref[place, pl.ds(at_low, BLK), :])
        high_ropes.append(rope_ref[place, pl.ds(at_high, BLK), :])
        low_blocks.append(jnp.minimum(first, second))
        high_blocks.append(jnp.maximum(first, second))
        low_at.append(at_low)
        high_at.append(at_high)
    low_keys = jnp.concatenate(low_keys, axis=0)
    high_keys = jnp.concatenate(high_keys, axis=0)
    low_ropes = jnp.concatenate(low_ropes, axis=0)
    high_ropes = jnp.concatenate(high_ropes, axis=0)

    ahead = (
        lax.broadcasted_iota(jnp.int32, (BLK, rows), 1) // heads
        - lax.broadcasted_iota(jnp.int32, (BLK, rows), 0)
    )

    def block(part, row_block, keys, ropes, key_blocks):
        q, qr, do = q_ref[part, :], qr_ref[part, :], do_ref[part, :]
        total, dots = tot_ref[:, part], dot_ref[:, part]
        scores = SOFTMAX_SCALE * (nt(keys, q) + nt(ropes, qr))
        probs = jnp.exp(scores - total)
        if key_blocks is not None:
            seen = jnp.concatenate(
                [ahead >= (b - row_block) * BLK for b in key_blocks], axis=0
            )
            probs = jnp.where(seen, probs, 0.0)
        dprobs = nt(keys, do)
        dscores = (SOFTMAX_SCALE * probs * (dprobs - dots)).astype(jnp.bfloat16)
        probs_low = probs.astype(jnp.bfloat16)
        return (
            tn(dscores, keys),
            tn(dscores, ropes),
            nn(dscores, q) + nn(probs_low, do),
            nn(dscores, qr),
        )

    gq_a, gqr_a, lat_a, rope_a = block(upper, high_mine, low_keys, low_ropes, None)
    gq_b, gqr_b, lat_b, rope_b = block(upper, high_mine, high_keys, high_ropes, high_blocks)
    gq_c, gqr_c, lat_c, rope_c = block(lower, low_mine, low_keys, low_ropes, low_blocks)
    gq_ref[upper, :] = (gq_a + gq_b).astype(jnp.bfloat16)
    gqr_ref[upper, :] = (gqr_a + gqr_b).astype(jnp.bfloat16)
    gq_ref[lower, :] = gq_c.astype(jnp.bfloat16)
    gqr_ref[lower, :] = gqr_c.astype(jnp.bfloat16)
    low_lat, low_rope = lat_a + lat_c, rope_a + rope_c
    blank = jnp.zeros((BLK, 64), jnp.float32)
    for place in range(SPAN):
        out_ref, base = (keep_ref, place) if place < 2 else (send_ref, place - 2)
        cut = slice(place * BLK, (place + 1) * BLK)
        for at, lat, rope in ((low_at, low_lat, low_rope), (high_at, lat_b, rope_b)):
            value = jnp.concatenate([lat[cut], rope[cut], blank], axis=1)
            out_ref[pl.ds(base * 2 * BLK + at[place], BLK), :] = value.astype(out_ref.dtype)


def attention(index, order, own, ka, kb, kc, q, qr, do, dots, totals):
    rows, width = q.shape
    vmem = pl.BlockSpec(memory_space=pltpu.VMEM)
    smem = pl.BlockSpec(memory_space=pltpu.SMEM)
    return pl.pallas_call(
        attention_kernel,
        out_shape=(
            jax.ShapeDtypeStruct((rows, width), jnp.bfloat16),
            jax.ShapeDtypeStruct((rows, 64), jnp.bfloat16),
            jax.ShapeDtypeStruct((256, 640), jnp.bfloat16),
            jax.ShapeDtypeStruct((256, 640), jnp.float32),
        ),
        in_specs=[smem, smem] + [vmem] * 9,
        out_specs=[vmem] * 4,
        scratch_shapes=[pltpu.VMEM((SPAN, 128, 64), jnp.bfloat16)],
        compiler_params=pltpu.CompilerParams(vmem_limit_bytes=48 * 2**20),
        cost_estimate=pl.CostEstimate(
            flops=3_000_000_000, bytes_accessed=5_000_000, transcendentals=400_000
        ),
    )(index, order, own, ka, kb, kc, q, qr, do, dots, totals)


def shards(q_lat, q_rope, d_out, latent, key_rope, forward_dot, log_total, block_order):
    tokens, heads, width = q_lat.shape
    rows = tokens * heads
    own = jnp.concatenate(
        [latent, jnp.concatenate([key_rope[16 * b : 16 * (b + 1)] for b in range(4)], axis=1)], axis=0
    )
    two_back = shift(own, 2)
    one_back = shift(own, 1)
    three_back = shift(two_back, 1)
    index = lax.axis_index("seq").astype(jnp.int32).reshape(1)
    grad_q, grad_qr, send, keep = attention(
        index,
        block_order,
        own,
        two_back,
        one_back,
        three_back,
        q_lat.reshape(rows, width),
        q_rope.reshape(rows, 64),
        d_out.reshape(rows, width),
        forward_dot.T.reshape(1, rows),
        log_total.T.reshape(1, rows),
    )
    near = shift(send, -1)
    far = shift((keep[128:] + near[128:].astype(jnp.float32)).astype(jnp.bfloat16), -2)
    mine = keep[:128] + near[:128].astype(jnp.float32) + far.astype(jnp.float32)
    parts = lax.all_to_all(mine.astype(jnp.bfloat16), "head", 0, 0, tiled=True)
    whole = parts.reshape(lax.axis_size("head"), -1, 640).astype(jnp.float32).sum(0)
    return (
        grad_q.reshape(tokens, heads, width),
        grad_qr.reshape(tokens, heads * 64),
        whole[:, :512].astype(jnp.bfloat16),
        whole[:, 512:576].astype(jnp.bfloat16),
    )


def solution(mesh):
    return jax.shard_map(
        shards,
        mesh=mesh,
        in_specs=(
            P("seq", "head", None),
            P("seq", "head"),
            P("seq", "head", None),
            P("seq", None),
            P(None, "seq"),
            P("head", "seq"),
            P("head", "seq"),
            P(),
        ),
        out_specs=(
            P("seq", "head", None),
            P("seq", "head"),
            P(("seq", "head"), None),
            P(("seq", "head"), None),
        ),
        check_vma=False,
    )
```

time: 384 us -> 82 us (0.21)
  waiting for transfers between devices: 255 us -> 26.9 us
  matrix products: 23.7 us -> 0 us
  starting transfers between devices: 61.3 us -> 39.7 us
  between operations: 20.8 us -> 0.73 us
  other arithmetic: 11.5 us -> 1.71 us
  Pallas kernels: 0 us -> 4.69 us
  local copies, waits for them, and re-layouts: 12.3 us -> 7.77 us
    unnamed x3 -> x0, waiting for transfers between devices: 114 us -> none
    reduce_scatter x1 -> x0, waiting for transfers between devices: 104 us -> none  [shards(): lax.psum_scatter(totals[0], 'head', scatter_dimension=0, tiled=True)]
    ppermute x14 -> x5, starting transfers between devices: 61.2 us -> 29.7 us  [shift(): return lax.ppermute(value, ('seq', 'head'), pairs)]
    ppermute x14 -> x5, waiting for transfers between devices: 37.4 us -> 13.4 us  [shift(): return lax.ppermute(value, ('seq', 'head'), pairs)]
    dot_general x32 -> x0, matrix products: 23.7 us -> none  [the longest x4 9.28 us: grad_tile(): jnp.einsum('kr,kd->rd', dscores, key_rows, preferred_element_type=jnp.flo...]
    all_to_all x0 -> x1, waiting for transfers between devices: none -> 13.5 us  [shards(): parts = lax.all_to_all(mine.astype(jnp.bfloat16), 'head', 0, 0, tiled=True)]
    all_to_all x0 -> x1, starting transfers between devices: none -> 9.99 us  [shards(): parts = lax.all_to_all(mine.astype(jnp.bfloat16), 'head', 0, 0, tiled=True)]
    add x7 -> x0, other arithmetic: 7.45 us -> none  [the longest x6 6.16 us: shards(): totals = (totals[0] + new_part[0], totals[1] + new_part[1])]
  transfers between devices with their start and end apart: 16 -> 6, of which waited for: 7 -> 5; matrix products, arithmetic and copies ran while one was open for 11% -> 2% of each run, Pallas kernels for 0% -> 0%
where the time goes in v1:
time: 82 us; the launch traced here: 81.5 us
  starting transfers between devices  39.7 us (48%)
  waiting for transfers between devices  26.9 us (33%)
  local copies, waits for them, and re-layouts  7.77 us (9%)
  Pallas kernels  4.69 us (6%)
  other arithmetic  1.71 us (2%)
    ppermute x5, starting transfers between devices, shift(): return lax.ppermute(value, ('seq', 'head'), pairs)  29.7 us
    all_to_all x1, waiting for transfers between devices, shards(): parts = lax.all_to_all(mine.astype(jnp.bfloat16), 'head', 0, 0, tiled=True)  13.5 us
    ppermute x5, waiting for transfers between devices, shift(): return lax.ppermute(value, ('seq', 'head'), pairs)  13.4 us
    all_to_all x1, starting transfers between devices, shards(): parts = lax.all_to_all(mine.astype(jnp.bfloat16), 'head', 0, 0, tiled=True)  9.99 us
    pallas_call x1, Pallas kernels, attention(): pl.pallas_call(attention_kernel, out_shape=(jax.ShapeDtypeStruct((rows, w...  4.69 us
    unnamed x12, local copies, waits for them, and re-layouts  4.37 us
  transfers between devices with their start and end apart: 6, of which 5 were waited for; matrix products, arithmetic and copies ran while one was open for 2% of the time, Pallas kernels for 0%

profile of v1, /device:TPU:1, one launch (start us, length us, event | category | flops | bytes accessed | tf_op | source)
XLA Modules:
  0.0 81.5 jit_solution(14645246351009541532)
XLA Ops:
  0.6 0.7 fusion
  1.4 0.9 %maximum_maximum_fusion.own_ref = bf16[144,512]{1,0:T(8,128)(2,1)S(1)} fusion(bf16[16,128]{1,0:T(8,128)(2,1)S(1)} %get-tuple-element.14, bf16[16,128]{1,0:T(8,128)(2,1)S(1)} %get-tuple-element.15, bf16[16,128]{1,0:T(8,128)(2,1)S(1)} %get-tuple-element.13, bf16[16,128]{1,0:T(8,128)(2,1)S(1)} %get-tuple-element.12, bf16[128,512]{1,0:T(8,128)(2,1)} %param.11), kind=kLoop, calls=%fused_computation.2 | loop fusion | flops 737280 | bytes 294912 | tf_op jit(solution)/shard_map/concatenate | solution.py:149
  2.3 4.4 %collective-permute-start = (bf16[144,512]{1,0:T(8,128)(2,1)S(1)}, bf16[144,512]{1,0:T(8,128)(2,1)S(1)}, u32[]{:S(2)}, u32[]{:S(2)}) collective-permute-start(bf16[144,512]{1,0:T(8,128)(2,1)S(1)} %maximum_maximum_fusion.own_ref), channel_id=1, source_target_pairs={{0,16},{1,17},{2,18},{3,19},{4,20},{5,21},{6,22},{7,23},{8,24},{9,... | collective-permute-start | bytes 442376 | tf_op jit(solution)/shard_map/ppermute | solution.py:22
  6.7 4.4 %collective-permute-start.1 = (bf16[144,512]{1,0:T(8,128)(2,1)S(1)}, bf16[144,512]{1,0:T(8,128)(2,1)S(1)}, u32[]{:S(2)}, u32[]{:S(2)}) collective-permute-start(bf16[144,512]{1,0:T(8,128)(2,1)S(1)} %maximum_maximum_fusion.own_ref), channel_id=1, source_target_pairs={{0,8},{1,9},{2,10},{3,11},{4,12},{5,13},{6,14},{7,15},{8,16},{9,17... | collective-permute-start | bytes 442376 | tf_op jit(solution)/shard_map/ppermute | solution.py:22
  11.1 8.9 %collective-permute-done.ka_ref = bf16[144,512]{1,0:T(8,128)(2,1)S(1)} collective-permute-done((bf16[144,512]{1,0:T(8,128)(2,1)S(1)}, bf16[144,512]{1,0:T(8,128)(2,1)S(1)}, u32[]{:S(2)}, u32[]{:S(2)}) %collective-permute-start) | collective-permute-done | bytes 147488 | tf_op jit(solution)/shard_map/ppermute | solution.py:22
  20.0 1.9 %collective-permute-start.2 = (bf16[144,512]{1,0:T(8,128)(2,1)S(1)}, bf16[144,512]{1,0:T(8,128)(2,1)S(1)}, u32[]{:S(2)}, u32[]{:S(2)}) collective-permute-start(bf16[144,512]{1,0:T(8,128)(2,1)S(1)} %collective-permute-done.ka_ref), channel_id=1, source_target_pairs={{0,8},{1,9},{2,10},{3,11},{4,12},{5,13},{6,14},{7,15},{8,16},{9,17... | collective-permute-start | bytes 442376 | tf_op jit(solution)/shard_map/ppermute | solution.py:22
  21.9 0.0 copy-start.4
  21.9 0.7 copy-done.4
  22.6 0.0 copy-start.3
  22.6 0.1 copy.14
  22.7 0.1 reshape.40.dot_ref
  22.8 0.6 copy-done.5
  23.4 0.1 copy.15
  23.5 0.1 reshape.41.tot_ref
  23.6 0.0 copy-done.3
  23.6 0.2 reshape.38.qr_ref
  23.8 0.0 collective-permute-done.1.kb_ref
  23.8 1.0 %collective-permute-done.2.kc_ref = bf16[144,512]{1,0:T(8,128)(2,1)S(1)} collective-permute-done((bf16[144,512]{1,0:T(8,128)(2,1)S(1)}, bf16[144,512]{1,0:T(8,128)(2,1)S(1)}, u32[]{:S(2)}, u32[]{:S(2)}) %collective-permute-start.2) | collective-permute-done | bytes 147488 | tf_op jit(solution)/shard_map/ppermute | solution.py:22
  24.8 0.7 copy-done.2
  25.5 1.2 %copy-done = bf16[128,8,512]{2,1,0:T(8,128)(2,1)S(1)} copy-done((bf16[128,8,512]{2,1,0:T(8,128)(2,1)S(1)}, bf16[128,8,512]{2,1,0:T(8,128)(2,1)}, u32[]{:S(2)}) %copy-start) | copy-done | bytes 1048600
  26.7 1.2 %copy-done.1 = bf16[128,8,512]{2,1,0:T(8,128)(2,1)S(1)} copy-done((bf16[128,8,512]{2,1,0:T(8,128)(2,1)S(1)}, bf16[128,8,512]{2,1,0:T(8,128)(2,1)}, u32[]{:S(2)}) %copy-start.1) | copy-done | bytes 1048600
  27.9 4.7 %shard_map.111 = (bf16[1024,512]{1,0:T(8,128)(2,1)}, bf16[1024,64]{1,0:T(8,128)(2,1)S(1)}, bf16[256,640]{1,0:T(8,128)(2,1)S(1)}, f32[256,640]{1,0:T(8,128)S(1)}) custom-call(s32[1]{0:T(128)} %bitcast.index_ref, s32[128]{0:T(128)S(1)} %copy-done.2, bf16[144,512]{1,0:T(8,128)(2,1)S(1)} %maximum_maximum_fusion.own_ref, ...), custom_call_target="tpu_custom_call" | custom-call | flops 3000000000 | bytes 5000000 | tf_op jit(solution)/shard_map/pallas_call | solution.py:128
  32.6 8.9 %collective-permute-start.3 = (bf16[256,640]{1,0:T(8,128)(2,1)S(1)}, bf16[256,640]{1,0:T(8,128)(2,1)S(1)}, u32[]{:S(2)}, u32[]{:S(2)}) collective-permute-start(bf16[256,640]{1,0:T(8,128)(2,1)S(1)} %get-tuple-element.11), channel_id=1, source_target_pairs={{0,505},{1,504},{2,507},{3,506},{4,509},{5,508},{6,511},{7,510},{8... | collective-permute-start | bytes 983048 | tf_op jit(solution)/shard_map/ppermute | solution.py:22
  41.5 1.2 %collective-permute-done.3 = bf16[256,640]{1,0:T(8,128)(2,1)S(1)} collective-permute-done((bf16[256,640]{1,0:T(8,128)(2,1)S(1)}, bf16[256,640]{1,0:T(8,128)(2,1)S(1)}, u32[]{:S(2)}, u32[]{:S(2)}) %collective-permute-start.3) | collective-permute-done | bytes 327712 | tf_op jit(solution)/shard_map/ppermute | solution.py:22
  42.8 10.1 %collective-permute-start.4 = (bf16[128,640]{1,0:T(8,128)(2,1)S(1)}, bf16[128,640]{1,0:T(8,128)(2,1)S(1)}, u32[]{:S(2)}, u32[]{:S(2)}) collective-permute-start(bf16[128,640]{1,0:T(8,128)(2,1)S(1)} %add_convert_fusion.1), channel_id=1, source_target_pairs={{0,497},{1,496},{2,499},{3,498},{4,501},{5,500},{6,503},{7,502},{8... | collective-permute-start | bytes 491528 | tf_op jit(solution)/shard_map/ppermute | solution.py:22
  52.9 2.2 %collective-permute-done.4 = bf16[128,640]{1,0:T(8,128)(2,1)S(1)} collective-permute-done((bf16[128,640]{1,0:T(8,128)(2,1)S(1)}, bf16[128,640]{1,0:T(8,128)(2,1)S(1)}, u32[]{:S(2)}, u32[]{:S(2)}) %collective-permute-start.4) | collective-permute-done | bytes 163872 | tf_op jit(solution)/shard_map/ppermute | solution.py:22
  55.1 0.7 add_convert_fusion
  55.9 10.0 %all-to-all-start = ((bf16[8,16,640]{2,1,0:T(8,128)(2,1)}), bf16[8,16,640]{2,1,0:T(8,128)(2,1)S(1)}, u32[]{:S(2)}, u32[]{:S(2)}) async-start(bf16[8,16,640]{2,1,0:T(8,128)(2,1)} %bitcast.6), calls=%async_computation | async-start | bytes 327680 | tf_op jit(solution)/shard_map/all_to_all | solution.py:172
  65.9 0.9 %reshape.43 = bf16[128,512]{1,0:T(8,128)(2,1)} reshape(bf16[1024,64]{1,0:T(8,128)(2,1)S(1)} %get-tuple-element.9) | data formatting | bytes 262144 | tf_op jit(solution)/shard_map/reshape | solution.py:176
  66.7 13.5 %all-to-all-done = bf16[8,16,640]{2,1,0:T(8,128)(2,1)S(1)} async-done(((bf16[8,16,640]{2,1,0:T(8,128)(2,1)}), bf16[8,16,640]{2,1,0:T(8,128)(2,1)S(1)}, u32[]{:S(2)}, u32[]{:S(2)}) %all-to-all-start) | async-done | bytes 163872 | tf_op jit(solution)/shard_map/all_to_all | solution.py:172
  80.3 0.6 slice.45
  80.9 0.6 slice.44
  (6 shorter events, 0.1 us)
Async XLA Ops:
  2.3 17.7 %collective-permute-start = (bf16[144,512]{1,0:T(8,128)(2,1)S(1)}, bf16[144,512]{1,0:T(8,128)(2,1)S(1)}, u32[]{:S(2)}, u32[]{:S(2)}) collective-permute-start(bf16[144,512]{1,0:T(8,128)(2,1)S(1)} %maximum_maximum_fusion.own_ref), channel_id=1, source_target_pairs={{0,16},{1,17},{2,18},{3,19},{4,20},{5,21},{6,22},{7,23},{8,24},{9,... | collective-permute-start | bytes 442376 | tf_op jit(solution)/shard_map/ppermute | solution.py:22
  6.7 17.1 %collective-permute-start.1 = (bf16[144,512]{1,0:T(8,128)(2,1)S(1)}, bf16[144,512]{1,0:T(8,128)(2,1)S(1)}, u32[]{:S(2)}, u32[]{:S(2)}) collective-permute-start(bf16[144,512]{1,0:T(8,128)(2,1)S(1)} %maximum_maximum_fusion.own_ref), channel_id=1, source_target_pairs={{0,8},{1,9},{2,10},{3,11},{4,12},{5,13},{6,14},{7,15},{8,16},{9,17... | collective-permute-start | bytes 442376 | tf_op jit(solution)/shard_map/ppermute | solution.py:22
  20.0 4.8 %collective-permute-start.2 = (bf16[144,512]{1,0:T(8,128)(2,1)S(1)}, bf16[144,512]{1,0:T(8,128)(2,1)S(1)}, u32[]{:S(2)}, u32[]{:S(2)}) collective-permute-start(bf16[144,512]{1,0:T(8,128)(2,1)S(1)} %collective-permute-done.ka_ref), channel_id=1, source_target_pairs={{0,8},{1,9},{2,10},{3,11},{4,12},{5,13},{6,14},{7,15},{8,16},{9,17... | collective-permute-start | bytes 442376 | tf_op jit(solution)/shard_map/ppermute | solution.py:22
  21.9 0.7 copy-start.4
  22.6 1.0 %copy-start.3 = (bf16[128,512]{1,0:T(8,128)(2,1)S(1)}, bf16[128,512]{1,0:T(8,128)(2,1)}, u32[]{:S(2)}) copy-start(bf16[128,512]{1,0:T(8,128)(2,1)} %param.9) | copy-start | bytes 393220
  22.7 0.7 copy-start.5
  24.8 0.7 copy-start.2
  25.5 1.2 %copy-start = (bf16[128,8,512]{2,1,0:T(8,128)(2,1)S(1)}, bf16[128,8,512]{2,1,0:T(8,128)(2,1)}, u32[]{:S(2)}) copy-start(bf16[128,8,512]{2,1,0:T(8,128)(2,1)} %param.8) | copy-start | bytes 3145732
  26.7 1.2 %copy-start.1 = (bf16[128,8,512]{2,1,0:T(8,128)(2,1)S(1)}, bf16[128,8,512]{2,1,0:T(8,128)(2,1)}, u32[]{:S(2)}) copy-start(bf16[128,8,512]{2,1,0:T(8,128)(2,1)} %param.10) | copy-start | bytes 3145732
  32.6 10.2 %collective-permute-start.3 = (bf16[256,640]{1,0:T(8,128)(2,1)S(1)}, bf16[256,640]{1,0:T(8,128)(2,1)S(1)}, u32[]{:S(2)}, u32[]{:S(2)}) collective-permute-start(bf16[256,640]{1,0:T(8,128)(2,1)S(1)} %get-tuple-element.11), channel_id=1, source_target_pairs={{0,505},{1,504},{2,507},{3,506},{4,509},{5,508},{6,511},{7,510},{8... | collective-permute-start | bytes 983048 | tf_op jit(solution)/shard_map/ppermute | solution.py:22
  42.8 12.3 %collective-permute-start.4 = (bf16[128,640]{1,0:T(8,128)(2,1)S(1)}, bf16[128,640]{1,0:T(8,128)(2,1)S(1)}, u32[]{:S(2)}, u32[]{:S(2)}) collective-permute-start(bf16[128,640]{1,0:T(8,128)(2,1)S(1)} %add_convert_fusion.1), channel_id=1, source_target_pairs={{0,497},{1,496},{2,499},{3,498},{4,501},{5,500},{6,503},{7,502},{8... | collective-permute-start | bytes 491528 | tf_op jit(solution)/shard_map/ppermute | solution.py:22
  55.9 24.4 %all-to-all-start = ((bf16[8,16,640]{2,1,0:T(8,128)(2,1)}), bf16[8,16,640]{2,1,0:T(8,128)(2,1)S(1)}, u32[]{:S(2)}, u32[]{:S(2)}) async-start(bf16[8,16,640]{2,1,0:T(8,128)(2,1)} %bitcast.6), calls=%async_computation | async-start | bytes 327680 | tf_op jit(solution)/shard_map/all_to_all | solution.py:172

commit v2 on v1

v2 whole, which is shorter than its diff:
```python
import jax
import jax.numpy as jnp
from jax import lax
from jax.experimental import pallas as pl
from jax.experimental.pallas import tpu as pltpu
from jax.sharding import PartitionSpec as P

SPAN = 4
SOFTMAX_SCALE = 192.0 ** (-0.5)
BLK = 64
RUN = 16
ORDER = (0, 2, 1, 3)


def permute(value, to):
    seqs, heads = lax.axis_size("seq"), lax.axis_size("head")
    pairs = []
    for i in range(seqs):
        if to(i) is None:
            continue
        j = to(i) % seqs
        for h in range(heads):
            pairs.append((i * heads + h, j * heads + (h ^ 1 if i // RUN != j // RUN else h)))
    return lax.ppermute(value, ("seq", "head"), pairs)


def shift(value, by):
    return permute(value, lambda i: i + by)


def swap_cores(value):
    return permute(value, lambda i: i ^ 1)


def nt(a, b):
    return lax.dot_general(a, b, (((1,), (1,)), ((), ())), preferred_element_type=jnp.float32)


def nn(a, b):
    return lax.dot_general(a, b, (((1,), (0,)), ((), ())), preferred_element_type=jnp.float32)


def tn(a, b):
    return lax.dot_general(a, b, (((0,), (0,)), ((), ())), preferred_element_type=jnp.float32)


def rope_of(packed):
    wide = jnp.concatenate([packed[:, 128 * b : 128 * (b + 1)] for b in range(4)], axis=0)
    return wide.astype(jnp.float32).T.astype(jnp.bfloat16)


def gather_keys(order_ref, me, shards_in_order, refs, bases, rope_ref):
    seqs = order_ref.shape[0] // 2
    low, high = [], []
    for place, s in enumerate(shards_in_order):
        other = lax.rem(me + seqs - s, seqs)
        first, second = order_ref[2 * other], order_ref[2 * other + 1]
        low_slot = jnp.where(first < second, 0, 1)
        at_low = pl.multiple_of(low_slot * BLK, BLK)
        at_high = pl.multiple_of((1 - low_slot) * BLK, BLK)
        rope_ref[place] = rope_of(refs[place][pl.ds(bases[place] + 2 * BLK, 16), :])
        for out, at, pos in ((low, at_low, jnp.minimum(first, second)), (high, at_high, jnp.maximum(first, second))):
            out.append((refs[place][pl.ds(pl.multiple_of(bases[place] + at, 16), BLK), :], rope_ref[place, pl.ds(at, BLK), :], pos, at))
    both = low + high
    keys = jnp.concatenate([x[0] for x in both], axis=0)
    ropes = jnp.concatenate([x[1] for x in both], axis=0)
    return keys, ropes, [x[2] for x in both], [x[3] for x in both]


def own_place(order_ref, me, rows):
    first, second = order_ref[2 * me], order_ref[2 * me + 1]
    high = jnp.where(first > second, 0, 1)
    upper = pl.multiple_of(high * rows, rows)
    lower = pl.multiple_of((1 - high) * rows, rows)
    return jnp.minimum(first, second), jnp.maximum(first, second), lower, upper


def tile(keys, ropes, key_blocks, row_block, q, qr, do, total, dots):
    rows = q.shape[0]
    scores = SOFTMAX_SCALE * (nt(keys, q) + nt(ropes, qr))
    probs = jnp.exp(scores - total)
    ahead = (
        lax.broadcasted_iota(jnp.int32, (BLK, rows), 1) // (rows // BLK)
        - lax.broadcasted_iota(jnp.int32, (BLK, rows), 0)
    )
    pieces = []
    for n, key_block in enumerate(key_blocks):
        piece = probs[n * BLK : (n + 1) * BLK]
        if key_block is not None:
            piece = jnp.where(ahead >= (key_block - row_block) * BLK, piece, 0.0)
        pieces.append(piece)
    probs = jnp.concatenate(pieces, axis=0)
    dprobs = nt(keys, do)
    dscores = (SOFTMAX_SCALE * probs * (dprobs - dots)).astype(jnp.bfloat16)
    return probs.astype(jnp.bfloat16), dscores


def pack_kernel(lat_hbm, rope_hbm, own_ref, sems):
    copies = [pltpu.make_async_copy(lat_hbm, own_ref.at[pl.ds(0, 128), :], sems.at[4])]
    for b in range(4):
        copies.append(
            pltpu.make_async_copy(
                rope_hbm.at[pl.ds(16 * b, 16), :],
                own_ref.at[pl.ds(128, 16), pl.ds(128 * b, 128)],
                sems.at[b],
            )
        )
    for copy in copies:
        copy.start()
    for copy in copies:
        copy.wait()


def spread(values):
    heads, tokens = values.shape
    rows = heads * tokens
    pieces, rest = [], values
    for _ in range(3):
        piece = rest.astype(jnp.bfloat16)
        rest = rest - piece.astype(jnp.float32)
        pieces.append(piece)
    column = lax.broadcasted_iota(jnp.int32, (tokens, rows), 1)
    token = lax.broadcasted_iota(jnp.int32, (tokens, rows), 0)
    pick = jnp.where(column // heads == token, 1.0, 0.0).astype(jnp.bfloat16)
    wide = (nn(pieces[0], pick) + nn(pieces[1], pick)) + nn(pieces[2], pick)
    column = lax.broadcasted_iota(jnp.int32, (heads, rows), 1)
    head = lax.broadcasted_iota(jnp.int32, (heads, rows), 0)
    return jnp.sum(jnp.where(lax.rem(column, heads) == head, wide, 0.0), axis=0, keepdims=True)


def prep_kernel(q_hbm, do_hbm, dot_ref, tot_ref, q_ref, do_ref, dots_ref, tots_ref, sems):
    copies = []
    rows = q_ref.shape[0] // 4
    for n in range(4):
        for m, (hbm, ref) in enumerate(((q_hbm, q_ref), (do_hbm, do_ref))):
            part = pl.ds(n * rows, rows)
            copies.append(pltpu.make_async_copy(hbm.at[part, :], ref.at[part, :], sems.at[n, m]))
    for copy in copies:
        copy.start()
    dots_ref[...] = spread(dot_ref[...])
    tots_ref[...] = spread(tot_ref[...])
    for copy in copies:
        copy.wait()


def early_kernel(
    order_ref, own_ref, ka_ref, q_ref, qr_ref, do_ref, dot_ref, tot_ref,
    ds_ref, lat_ref, grope_ref, keys_ref, ropes_ref,
    rope_ref,
):
    me = lax.axis_index("seq")
    rows = q_ref.shape[0] // 2
    _, high_mine, _, upper = own_place(order_ref, me, rows)
    part = pl.ds(upper, rows)
    keys, ropes, blocks, _ = gather_keys(order_ref, me, ORDER[:2], (own_ref, ka_ref), (0, 0), rope_ref)
    keys_ref[...] = keys
    ropes_ref[...] = ropes
    q, qr, do = q_ref[part, :], qr_ref[part, :], do_ref[part, :]
    probs, ds = tile(
        keys, ropes, [None, None] + blocks[2:], high_mine, q, qr, do, tot_ref[:, part], dot_ref[:, part]
    )
    ds_ref[...] = ds
    lat_ref[...] = nn(ds, q) + nn(probs, do)
    grope_ref[...] = nn(ds, qr)


def main_kernel(
    order_ref, pair_ref, three_ref, q_ref, qr_ref, do_ref, dot_ref, tot_ref, lat_ref, grope_ref, keys_a_ref, ropes_a_ref,
    sib_ref, far_ref, keep_ref, ds_b_ref, ds_c_ref, keys_b_ref, ropes_b_ref,
    rope_ref,
):
    me = lax.axis_index("seq")
    even = lax.rem(me, 2) == 0
    rows = q_ref.shape[0] // 2
    low_mine, high_mine, lower, upper = own_place(order_ref, me, rows)
    seqs = order_ref.shape[0] // 2
    keys, ropes, blocks, at_b = gather_keys(
        order_ref, me, ORDER[2:], (pair_ref, three_ref), (0, 0), rope_ref
    )
    keys_b_ref[...] = keys
    ropes_b_ref[...] = ropes
    low_blocks, at_a = [], []
    for s in ORDER[:2]:
        other = lax.rem(me + seqs - s, seqs)
        first, second = order_ref[2 * other], order_ref[2 * other + 1]
        low_blocks.append(jnp.minimum(first, second))
        at_a.append(pl.multiple_of(jnp.where(first < second, 0, BLK), BLK))
    at_a += [pl.multiple_of(BLK - at, BLK) for at in at_a]
    low_keys = jnp.concatenate([keys_a_ref[: 2 * BLK], keys[: 2 * BLK]], axis=0)
    low_ropes = jnp.concatenate([ropes_a_ref[: 2 * BLK], ropes[: 2 * BLK]], axis=0)

    part = pl.ds(upper, rows)
    q, qr, do = q_ref[part, :], qr_ref[part, :], do_ref[part, :]
    probs, ds = tile(
        keys, ropes, [None, None] + blocks[2:], high_mine, q, qr, do, tot_ref[:, part], dot_ref[:, part]
    )
    ds_b_ref[...] = ds
    lat_b = nn(ds, q) + nn(probs, do)
    grope_b = nn(ds, qr)

    part = pl.ds(lower, rows)
    q, qr, do = q_ref[part, :], qr_ref[part, :], do_ref[part, :]
    probs, ds = tile(
        low_keys, low_ropes, low_blocks + blocks[:2], low_mine, q, qr, do, tot_ref[:, part], dot_ref[:, part]
    )
    ds_c_ref[...] = ds
    lat_c = nn(ds, q) + nn(probs, do)
    grope_c = nn(ds, qr)

    half = 2 * BLK
    blank = jnp.zeros((BLK, 64), jnp.float32)

    def whole(lat, grope, more, n):
        cut = slice(n * BLK, (n + 1) * BLK)
        lat_n, grope_n = lat[cut], grope[cut]
        if n < 2:
            add = slice(more + n * BLK, more + (n + 1) * BLK)
            lat_n, grope_n = lat_n + lat_c[add], grope_n + grope_c[add]
        return jnp.concatenate([lat_n, grope_n, blank], axis=1)

    lat_a, grope_a = lat_ref[...], grope_ref[...]
    for n, at in enumerate(at_a):
        keep_ref[pl.ds((n % 2) * half + at, BLK), :] = whole(lat_a, grope_a, 0, n)
    for n in (0, 2):
        one = whole(lat_b, grope_b, half, n)
        three = whole(lat_b, grope_b, half, n + 1)
        far_ref[pl.ds(at_b[n + 1], BLK), :] = three.astype(jnp.bfloat16)
        sib_ref[pl.ds(at_b[n], BLK), :] = jnp.where(even, 0.0, one).astype(jnp.bfloat16)
        second = half + jnp.where(even, at_b[n], at_b[n + 1])
        sib_ref[pl.ds(pl.multiple_of(second, BLK), BLK), :] = jnp.where(even, one, three).astype(jnp.bfloat16)


def query_kernel(
    order_ref, ds_a_ref, ds_b_ref, ds_c_ref, keys_a_ref, ropes_a_ref, keys_b_ref, ropes_b_ref, gq_ref, gqr_ref
):
    me = lax.axis_index("seq")
    rows = ds_a_ref.shape[1]
    _, _, lower, upper = own_place(order_ref, me, rows)
    half = 2 * BLK
    low_keys = jnp.concatenate([keys_a_ref[:half], keys_b_ref[:half]], axis=0)
    low_ropes = jnp.concatenate([ropes_a_ref[:half], ropes_b_ref[:half]], axis=0)
    ds_a, ds_b, ds_c = ds_a_ref[...], ds_b_ref[...], ds_c_ref[...]
    part = pl.ds(upper, rows)
    gq_ref[part, :] = (tn(ds_a, keys_a_ref[...]) + tn(ds_b, keys_b_ref[...])).astype(jnp.bfloat16)
    gqr_ref[part, :] = (tn(ds_a, ropes_a_ref[...]) + tn(ds_b, ropes_b_ref[...])).astype(jnp.bfloat16)
    part = pl.ds(lower, rows)
    gq_ref[part, :] = tn(ds_c, low_keys).astype(jnp.bfloat16)
    gqr_ref[part, :] = tn(ds_c, low_ropes).astype(jnp.bfloat16)


VMEM = pl.BlockSpec(memory_space=pltpu.VMEM)
SMEM = pl.BlockSpec(memory_space=pltpu.SMEM)
HBM = pl.BlockSpec(memory_space=pltpu.HBM)


def in_hbm(value):
    return pltpu.with_memory_space_constraint(value, pltpu.HBM)


def call(kernel, args, in_specs, outs, scratch, gflop, aliases={}):
    return pl.pallas_call(
        kernel,
        out_shape=tuple(jax.ShapeDtypeStruct(shape, dtype) for shape, dtype in outs),
        in_specs=in_specs,
        out_specs=(VMEM,) * len(outs),
        scratch_shapes=scratch,
        input_output_aliases=aliases,
        compiler_params=pltpu.CompilerParams(vmem_limit_bytes=32 * 2**20),
        cost_estimate=pl.CostEstimate(
            flops=int(gflop * 1e9), bytes_accessed=int(gflop * 2e6), transcendentals=int(gflop * 1e5)
        ),
    )(*args)


def share_kernel(parts_ref, keep_ref, send_ref):
    whole = parts_ref[0].astype(jnp.float32)
    for n in range(1, parts_ref.shape[0]):
        whole = whole + parts_ref[n].astype(jnp.float32)
    rows = keep_ref.shape[0]
    first = lax.rem(lax.axis_index("head"), 2) == 0
    keep_ref[...] = jnp.where(first, whole[:rows], whole[rows:])
    send_ref[...] = jnp.where(first, whole[rows:], whole[:rows]).astype(jnp.bfloat16)


def last_kernel(keep_ref, got_ref, lat_ref, rope_ref):
    whole = keep_ref[...] + got_ref[...].astype(jnp.float32)
    lat_ref[...] = whole[:, :512].astype(jnp.bfloat16)
    rope_ref[...] = whole[:, 512:576].astype(jnp.bfloat16)


def shards(q_lat, q_rope, d_out, latent, key_rope, forward_dot, log_total, block_order):
    tokens, heads, width = q_lat.shape
    rows = tokens * heads
    half, bf16, f32 = rows // 2, jnp.bfloat16, jnp.float32
    (own,) = call(
        pack_kernel,
        (in_hbm(latent), in_hbm(key_rope)),
        [HBM] * 2,
        [((tokens + 16, width), bf16)],
        [pltpu.SemaphoreType.DMA((5,))],
        0.0,
    )
    two_back = shift(own, 2)
    q, do, dots, sums = call(
        prep_kernel,
        (in_hbm(q_lat.reshape(rows, width)), in_hbm(d_out.reshape(rows, width)), forward_dot, log_total),
        [HBM, HBM, VMEM, VMEM],
        [((rows, width), bf16), ((rows, width), bf16), ((1, rows), f32), ((1, rows), f32)],
        [pltpu.SemaphoreType.DMA((4, 2))],
        0.0,
    )
    qr = q_rope.reshape(rows, 64)
    two_back, q, do, dots, sums, qr = lax.optimization_barrier((two_back, q, do, dots, sums, qr))
    three_back = shift(two_back, 1)
    pair = shift(own, 1)
    ds_a, lat_a, grope_a, keys_a, ropes_a = call(
        early_kernel,
        (block_order, own, two_back, q, qr, do, dots, sums),
        [SMEM] + [VMEM] * 7,
        [((256, half), bf16), ((256, width), f32), ((256, 64), f32), ((256, width), bf16), ((256, 64), bf16)],
        [pltpu.VMEM((2, 128, 64), bf16)],
        0.0,
    )
    sib, far, keep, ds_b, ds_c, keys_b, ropes_b = call(
        main_kernel,
        (block_order, pair, three_back, q, qr, do, dots, sums, lat_a, grope_a, keys_a, ropes_a),
        [SMEM] + [VMEM] * 11,
        [
            ((256, 640), bf16),
            ((128, 640), bf16),
            ((256, 640), f32),
            ((256, half), bf16),
            ((256, half), bf16),
            ((256, width), bf16),
            ((256, 64), bf16),
        ],
        [pltpu.VMEM((2, 128, 64), bf16)],
        1.6,
    )
    near = swap_cores(sib)
    from_three = permute(far, lambda i: None if i % 2 else i - 3)
    grad_q, grad_qr = call(
        query_kernel,
        (block_order, ds_a, ds_b, ds_c, keys_a, ropes_a, keys_b, ropes_b),
        [SMEM] + [VMEM] * 7,
        [((rows, width), bf16), ((rows, 64), bf16)],
        [],
        0.8,
    )
    grad_qr = grad_qr.reshape(tokens, heads * 64)
    near = near.astype(f32)
    from_two = shift((keep[128:] + near[128:]).astype(bf16), -2)
    mine = (keep[:128] + near[:128] + from_three.astype(f32) + from_two.astype(f32)).astype(bf16)
    mine, grad_qr = lax.optimization_barrier((mine, grad_qr))
    parts = lax.all_to_all(
        mine, "head", 0, 0, tiled=True, axis_index_groups=[[0, 2, 4, 6], [1, 3, 5, 7]]
    ).reshape(4, tokens // 4, 640)
    share = tokens // 8
    kept, given = call(
        share_kernel, (parts,), [VMEM], [((share, 640), f32), ((share, 640), bf16)], [], 0.01
    )
    got = lax.ppermute(given, "head", [(h, h ^ 1) for h in range(8)])
    lat_grad, rope_grad = call(
        last_kernel, (kept, got), [VMEM] * 2, [((share, width), bf16), ((share, 64), bf16)], [], 0.01
    )
    return grad_q.reshape(tokens, heads, width), grad_qr, lat_grad, rope_grad


def solution(mesh):
    return jax.shard_map(
        shards,
        mesh=mesh,
        in_specs=(
            P("seq", "head", None),
            P("seq", "head"),
            P("seq", "head", None),
            P("seq", None),
            P(None, "seq"),
            P("head", "seq"),
            P("head", "seq"),
            P(),
        ),
        out_specs=(
            P("seq", "head", None),
            P("seq", "head"),
            P(("seq", "head"), None),
            P(("seq", "head"), None),
        ),
        check_vma=False,
    )
```

time: 82 us -> 70.7 us (0.86)
  waiting for transfers between devices: 26.9 us -> 17.9 us
  blocking collectives: 0 us -> 8.98 us
  starting transfers between devices: 39.7 us -> 30.9 us
  local copies, waits for them, and re-layouts: 7.77 us -> 1.56 us
  Pallas kernels: 4.69 us -> 9.42 us
  other arithmetic: 1.71 us -> 0.14 us
    all_to_all x1 -> x0, waiting for transfers between devices: 13.5 us -> none  [shards(): parts = lax.all_to_all(mine.astype(jnp.bfloat16), 'head', 0, 0, tiled=True)]
    all_to_all x1 -> x0, starting transfers between devices: 9.99 us -> none  [shards(): parts = lax.all_to_all(mine.astype(jnp.bfloat16), 'head', 0, 0, tiled=True)]
    all_to_all x0 -> x1, blocking collectives: none -> 8.98 us  [shards(): lax.all_to_all(mine, 'head', 0, 0, tiled=True, axis_index_groups=[[0, 2,...]
    pallas_call x1 -> x7, Pallas kernels: 4.69 us -> 9.42 us  [call(): pl.pallas_call(kernel, out_shape=tuple((jax.ShapeDtypeStruct(shape, dtype...]
    ppermute x5 -> x7, waiting for transfers between devices: 13.4 us -> 17.9 us  [the longest x6 12.6 us: permute(): return lax.ppermute(value, ('seq', 'head'), pairs)]
    unnamed x12 -> x8, local copies, waits for them, and re-layouts: 4.37 us -> 0.51 us
    slice x3 -> x0, local copies, waits for them, and re-layouts: 1.94 us -> none  [the longest x1 0.74 us: shards(): key_rope[16 * b:16 * (b + 1)]]
    ppermute x5 -> x7, starting transfers between devices: 29.7 us -> 30.9 us  [the longest x6 22.9 us: permute(): return lax.ppermute(value, ('seq', 'head'), pairs)]
  transfers between devices with their start and end apart: 6 -> 7, of which waited for: 5 -> 5; matrix products, arithmetic and copies ran while one was open for 2% -> 2% of each run, Pallas kernels for 0% -> 8%
where the time goes in v2:
time: 70.7 us; the launch traced here: 69.7 us
  starting transfers between devices  30.9 us (44%)
  waiting for transfers between devices  17.9 us (25%)
  Pallas kernels  9.42 us (13%)
  blocking collectives  8.98 us (13%)
  local copies, waits for them, and re-layouts  1.56 us (2%)
  between operations  0.81 us (1%)
    ppermute x6, starting transfers between devices, permute(): return lax.ppermute(value, ('seq', 'head'), pairs)  22.9 us
    ppermute x6, waiting for transfers between devices, permute(): return lax.ppermute(value, ('seq', 'head'), pairs)  12.6 us
    pallas_call x7, Pallas kernels, call(): pl.pallas_call(kernel, out_shape=tuple((jax.ShapeDtypeStruct(shape, dtype...  9.42 us
    all_to_all x1, blocking collectives, shards(): lax.all_to_all(mine, 'head', 0, 0, tiled=True, axis_index_groups=[[0, 2,...  8.98 us
    ppermute x1, starting transfers between devices, shards(): got = lax.ppermute(given, 'head', [(h, h ^ 1) for h in range(8)])  7.97 us
    ppermute x1, waiting for transfers between devices, shards(): got = lax.ppermute(given, 'head', [(h, h ^ 1) for h in range(8)])  5.32 us
  transfers between devices with their start and end apart: 7, of which 5 were waited for; matrix products, arithmetic and copies ran while one was open for 2% of the time, Pallas kernels for 8%

profile of v2, /device:TPU:1, one launch (start us, length us, event | category | flops | bytes accessed | tf_op | source)
XLA Modules:
  0.0 69.7 jit_solution(15107377604497917228)
XLA Ops:
  0.6 0.0 copy-start.3
  0.6 1.0 %shard_map.111.own_ref = bf16[144,512]{1,0:T(8,128)(2,1)S(1)} custom-call(bf16[128,512]{1,0:T(8,128)(2,1)} %lat_hbm.1, bf16[64,128]{1,0:T(8,128)(2,1)} %rope_hbm.1), custom_call_target="tpu_custom_call" | custom-call | tf_op jit(solution)/shard_map/pallas_call | solution.py:261
  1.6 4.4 %collective-permute-start = (bf16[144,512]{1,0:T(8,128)(2,1)S(1)}, bf16[144,512]{1,0:T(8,128)(2,1)S(1)}, u32[]{:S(2)}, u32[]{:S(2)}) collective-permute-start(bf16[144,512]{1,0:T(8,128)(2,1)S(1)} %shard_map.111.own_ref), channel_id=1, source_target_pairs={{0,16},{1,17},{2,18},{3,19},{4,20},{5,21},{6,22},{7,23},{8,24},{9,... | collective-permute-start | bytes 442376 | tf_op jit(solution)/shard_map/ppermute | solution.py:24
  6.0 4.4 %collective-permute-start.1 = (bf16[144,512]{1,0:T(8,128)(2,1)S(1)}, bf16[144,512]{1,0:T(8,128)(2,1)S(1)}, u32[]{:S(2)}, u32[]{:S(2)}) collective-permute-start(bf16[144,512]{1,0:T(8,128)(2,1)S(1)} %shard_map.111.own_ref), channel_id=1, source_target_pairs={{0,8},{1,9},{2,10},{3,11},{4,12},{5,13},{6,14},{7,15},{8,16},{9,17... | collective-permute-start | bytes 442376 | tf_op jit(solution)/shard_map/ppermute | solution.py:24
  10.4 0.0 copy-done.3
  10.4 0.0 copy-start
  10.4 0.0 copy-start.1
  10.5 0.2 reshape.29.qr_ref
  10.6 0.5 copy-done
  11.1 0.0 copy-done.1
  11.1 1.6 %shard_map.112 = (bf16[1024,512]{1,0:T(8,128)(2,1)S(1)}, bf16[1024,512]{1,0:T(8,128)(2,1)S(1)}, f32[1,1024]{1,0:T(1,128)S(1)}, f32[1,1024]{1,0:T(1,128)S(1)}) custom-call(bf16[1024,512]{1,0:T(8,128)(2,1)} %bitcast.4, bf16[1024,512]{1,0:T(8,128)(2,1)} %bitcast.5, f32[8,128]{1,0:T(8,128)S(1)} %copy-done, f32[8,128]{1,0:T(8,128)S(1)} %copy-done.1), custom_call_target="tpu_custom_call" | custom-call | tf_op jit(solution)/shard_map/pallas_call | solution.py:261
  12.7 6.6 %collective-permute-done.ka_ref = bf16[144,512]{1,0:T(8,128)(2,1)S(1)} collective-permute-done((bf16[144,512]{1,0:T(8,128)(2,1)S(1)}, bf16[144,512]{1,0:T(8,128)(2,1)S(1)}, u32[]{:S(2)}, u32[]{:S(2)}) %collective-permute-start) | collective-permute-done | bytes 147488 | tf_op jit(solution)/shard_map/ppermute | solution.py:24
  19.4 0.0 copy-start.2
  19.4 2.0 %collective-permute-start.2 = (bf16[144,512]{1,0:T(8,128)(2,1)S(1)}, bf16[144,512]{1,0:T(8,128)(2,1)S(1)}, u32[]{:S(2)}, u32[]{:S(2)}) collective-permute-start(bf16[144,512]{1,0:T(8,128)(2,1)S(1)} %collective-permute-done.ka_ref), channel_id=1, source_target_pairs={{0,8},{1,9},{2,10},{3,11},{4,12},{5,13},{6,14},{7,15},{8,16},{9,17... | collective-permute-start | bytes 442376 | tf_op jit(solution)/shard_map/ppermute | solution.py:24
  21.4 0.0 copy-done.2
  21.4 1.5 %shard_map.113 = (bf16[256,512]{1,0:T(8,128)(2,1)S(1)}, f32[256,512]{1,0:T(8,128)S(1)}, f32[256,64]{1,0:T(8,128)S(1)}, bf16[256,512]{1,0:T(8,128)(2,1)S(1)}, bf16[256,64]{1,0:T(8,128)(2,1)S(1)}) custom-call(s32[128]{0:T(128)S(1)} %copy-done.2, bf16[144,512]{1,0:T(8,128)(2,1)S(1)} %shard_map.111.own_ref, bf16[144,512]{1,0:T(8,128)(2,1)S(1)} %collective-permute-done.ka_ref, ...), custom_call_target="tpu_custom_call" | custom-call | tf_op jit(solution)/shard_map/pallas_call | solution.py:261
  23.0 0.0 collective-permute-done.1.pair_ref
  23.0 1.3 %collective-permute-done.2.three_ref = bf16[144,512]{1,0:T(8,128)(2,1)S(1)} collective-permute-done((bf16[144,512]{1,0:T(8,128)(2,1)S(1)}, bf16[144,512]{1,0:T(8,128)(2,1)S(1)}, u32[]{:S(2)}, u32[]{:S(2)}) %collective-permute-start.2) | collective-permute-done | bytes 147488 | tf_op jit(solution)/shard_map/ppermute | solution.py:24
  24.3 2.4 %shard_map.114 = (bf16[256,640]{1,0:T(8,128)(2,1)S(1)}, bf16[128,640]{1,0:T(8,128)(2,1)S(1)}, f32[256,640]{1,0:T(8,128)S(1)}, bf16[256,512]{1,0:T(8,128)(2,1)S(1...) custom-call(s32[128]{0:T(128)S(1)} %copy-done.2, ...), custom_call_target="tpu_custom_call" | custom-call | flops 1600000000 | bytes 3200000 | tf_op jit(solution)/shard_map/pallas_call | solution.py:261
  26.7 8.9 %collective-permute-start.3 = (bf16[256,640]{1,0:T(8,128)(2,1)S(1)}, bf16[256,640]{1,0:T(8,128)(2,1)S(1)}, u32[]{:S(2)}, u32[]{:S(2)}) collective-permute-start(bf16[256,640]{1,0:T(8,128)(2,1)S(1)} %get-tuple-element.55), channel_id=1, source_target_pairs={{0,8},{1,9},{2,10},{3,11},{4,12},{5,13},{6,14},{7,15},{8,0},{9,1},... | collective-permute-start | bytes 983048 | tf_op jit(solution)/shard_map/ppermute | solution.py:24
  35.6 1.3 %collective-permute-start.4 = (bf16[128,640]{1,0:T(8,128)(2,1)S(1)}, bf16[128,640]{1,0:T(8,128)(2,1)S(1)}, u32[]{:S(2)}, u32[]{:S(2)}) collective-permute-start(bf16[128,640]{1,0:T(8,128)(2,1)S(1)} %get-tuple-element.56), channel_id=1, source_target_pairs={{0,489},{1,488},{2,491},{3,490},{4,493},{5,492},{6,495},{7,494},{1... | collective-permute-start | bytes 491528 | tf_op jit(solution)/shard_map/ppermute | solution.py:24
  36.9 0.0 collective-permute-done.3
  37.0 1.9 %collective-permute-start.5 = (bf16[128,640]{1,0:T(8,128)(2,1)S(1)}, bf16[128,640]{1,0:T(8,128)(2,1)S(1)}, u32[]{:S(2)}, u32[]{:S(2)}) collective-permute-start(bf16[128,640]{1,0:T(8,128)(2,1)S(1)} %fusion), channel_id=1, source_target_pairs={{0,497},{1,496},{2,499},{3,498},{4,501},{5,500},{6,503},{7,502},{8... | collective-permute-start | bytes 491528 | tf_op jit(solution)/shard_map/ppermute | solution.py:24
  38.9 2.3 %shard_map.115 = (bf16[1024,512]{1,0:T(8,128)(2,1)}, bf16[1024,64]{1,0:T(8,128)(2,1)S(1)}) custom-call(s32[128]{0:T(128)S(1)} %copy-done.2, bf16[256,512]{1,0:T(8,128)(2,1)S(1)} %get-tuple-element.44.ds_a_ref, bf16[256,512]{1,0:T(8,128)(2,1)S(1)} %get-tuple-element.49.ds_b_ref, bf16[256,512]{1,0:T(8,128)(2,1)S(1)} %get-tuple-element.50.ds_c_ref, ...), custom_call_target="tpu_custom_call" | custom-call | flops 800000000 | bytes 1600000 | tf_op jit(solution)/shard_map/pallas_call | solution.py:261
  41.2 0.9 %reshape.31 = bf16[128,512]{1,0:T(8,128)(2,1)} reshape(bf16[1024,64]{1,0:T(8,128)(2,1)S(1)} %get-tuple-element.57) | data formatting | bytes 262144 | tf_op jit(solution)/shard_map/reshape | solution.py:350
  42.1 1.1 %collective-permute-done.4 = bf16[128,640]{1,0:T(8,128)(2,1)S(1)} collective-permute-done((bf16[128,640]{1,0:T(8,128)(2,1)S(1)}, bf16[128,640]{1,0:T(8,128)(2,1)S(1)}, u32[]{:S(2)}, u32[]{:S(2)}) %collective-permute-start.4) | collective-permute-done | bytes 163872 | tf_op jit(solution)/shard_map/ppermute | solution.py:24
  43.2 3.5 %collective-permute-done.5 = bf16[128,640]{1,0:T(8,128)(2,1)S(1)} collective-permute-done((bf16[128,640]{1,0:T(8,128)(2,1)S(1)}, bf16[128,640]{1,0:T(8,128)(2,1)S(1)}, u32[]{:S(2)}, u32[]{:S(2)}) %collective-permute-start.5) | collective-permute-done | bytes 163872 | tf_op jit(solution)/shard_map/ppermute | solution.py:24
  46.7 0.1 fusion.3
  46.8 9.0 %all_to_all.9.parts_ref = bf16[4,32,640]{2,1,0:T(8,128)(2,1)S(1)} all-to-all(bf16[4,32,640]{2,1,0:T(8,128)(2,1)S(1)} %bitcast.6), channel_id=1, replica_groups={{0,2,4,6},{1,3,5,7},{8,10,12,14},{9,11,13,15},{16,18,20,22},{17,19,21,2..., dimensions={0} | all-to-all | bytes 327680 | tf_op jit(solution)/shard_map/all_to_all | solution.py:355
  55.8 8.0 %collective-permute-start.6 = (bf16[16,640]{1,0:T(8,128)(2,1)S(1)}, bf16[16,640]{1,0:T(8,128)(2,1)S(1)}, u32[]{:S(2)}, u32[]{:S(2)}) collective-permute-start(bf16[16,640]{1,0:T(8,128)(2,1)S(1)} %get-tuple-element.61), channel_id=1, source_target_pairs={{0,1},{1,0},{2,3},{3,2},{4,5},{5,4},{6,7},{7,6},{8,9},{9,8},{10,11... | collective-permute-start | bytes 61448 | tf_op jit(solution)/shard_map/ppermute | solution.py:362
  63.8 5.3 %collective-permute-done.6.got_ref = bf16[16,640]{1,0:T(8,128)(2,1)S(1)} collective-permute-done((bf16[16,640]{1,0:T(8,128)(2,1)S(1)}, bf16[16,640]{1,0:T(8,128)(2,1)S(1)}, u32[]{:S(2)}, u32[]{:S(2)}) %collective-permute-start.6) | collective-permute-done | bytes 20512 | tf_op jit(solution)/shard_map/ppermute | solution.py:362
  69.1 0.6 shard_map.117
  (3 shorter events, 0.1 us)
Async XLA Ops:
  0.6 9.8 %copy-start.3 = (bf16[128,512]{1,0:T(8,128)(2,1)S(1)}, bf16[128,512]{1,0:T(8,128)(2,1)}, u32[]{:S(2)}) copy-start(bf16[128,512]{1,0:T(8,128)(2,1)} %param.9) | copy-start | bytes 393220
  1.6 17.7 %collective-permute-start = (bf16[144,512]{1,0:T(8,128)(2,1)S(1)}, bf16[144,512]{1,0:T(8,128)(2,1)S(1)}, u32[]{:S(2)}, u32[]{:S(2)}) collective-permute-start(bf16[144,512]{1,0:T(8,128)(2,1)S(1)} %shard_map.111.own_ref), channel_id=1, source_target_pairs={{0,16},{1,17},{2,18},{3,19},{4,20},{5,21},{6,22},{7,23},{8,24},{9,... | collective-permute-start | bytes 442376 | tf_op jit(solution)/shard_map/ppermute | solution.py:24
  6.0 16.9 %collective-permute-start.1 = (bf16[144,512]{1,0:T(8,128)(2,1)S(1)}, bf16[144,512]{1,0:T(8,128)(2,1)S(1)}, u32[]{:S(2)}, u32[]{:S(2)}) collective-permute-start(bf16[144,512]{1,0:T(8,128)(2,1)S(1)} %shard_map.111.own_ref), channel_id=1, source_target_pairs={{0,8},{1,9},{2,10},{3,11},{4,12},{5,13},{6,14},{7,15},{8,16},{9,17... | collective-permute-start | bytes 442376 | tf_op jit(solution)/shard_map/ppermute | solution.py:24
  10.4 0.7 copy-start
  10.4 0.7 copy-start.1
  19.4 2.1 %copy-start.2 = (s32[128]{0:T(128)S(1)}, s32[128]{0:T(128)}, u32[]{:S(2)}) copy-start(s32[128]{0:T(128)} %order_ref.5) | copy-start | bytes 1540
  19.4 4.9 %collective-permute-start.2 = (bf16[144,512]{1,0:T(8,128)(2,1)S(1)}, bf16[144,512]{1,0:T(8,128)(2,1)S(1)}, u32[]{:S(2)}, u32[]{:S(2)}) collective-permute-start(bf16[144,512]{1,0:T(8,128)(2,1)S(1)} %collective-permute-done.ka_ref), channel_id=1, source_target_pairs={{0,8},{1,9},{2,10},{3,11},{4,12},{5,13},{6,14},{7,15},{8,16},{9,17... | collective-permute-start | bytes 442376 | tf_op jit(solution)/shard_map/ppermute | solution.py:24
  26.7 10.2 %collective-permute-start.3 = (bf16[256,640]{1,0:T(8,128)(2,1)S(1)}, bf16[256,640]{1,0:T(8,128)(2,1)S(1)}, u32[]{:S(2)}, u32[]{:S(2)}) collective-permute-start(bf16[256,640]{1,0:T(8,128)(2,1)S(1)} %get-tuple-element.55), channel_id=1, source_target_pairs={{0,8},{1,9},{2,10},{3,11},{4,12},{5,13},{6,14},{7,15},{8,0},{9,1},... | collective-permute-start | bytes 983048 | tf_op jit(solution)/shard_map/ppermute | solution.py:24
  35.6 7.6 %collective-permute-start.4 = (bf16[128,640]{1,0:T(8,128)(2,1)S(1)}, bf16[128,640]{1,0:T(8,128)(2,1)S(1)}, u32[]{:S(2)}, u32[]{:S(2)}) collective-permute-start(bf16[128,640]{1,0:T(8,128)(2,1)S(1)} %get-tuple-element.56), channel_id=1, source_target_pairs={{0,489},{1,488},{2,491},{3,490},{4,493},{5,492},{6,495},{7,494},{1... | collective-permute-start | bytes 491528 | tf_op jit(solution)/shard_map/ppermute | solution.py:24
  37.0 9.7 %collective-permute-start.5 = (bf16[128,640]{1,0:T(8,128)(2,1)S(1)}, bf16[128,640]{1,0:T(8,128)(2,1)S(1)}, u32[]{:S(2)}, u32[]{:S(2)}) collective-permute-start(bf16[128,640]{1,0:T(8,128)(2,1)S(1)} %fusion), channel_id=1, source_target_pairs={{0,497},{1,496},{2,499},{3,498},{4,501},{5,500},{6,503},{7,502},{8... | collective-permute-start | bytes 491528 | tf_op jit(solution)/shard_map/ppermute | solution.py:24
  55.8 13.3 %collective-permute-start.6 = (bf16[16,640]{1,0:T(8,128)(2,1)S(1)}, bf16[16,640]{1,0:T(8,128)(2,1)S(1)}, u32[]{:S(2)}, u32[]{:S(2)}) collective-permute-start(bf16[16,640]{1,0:T(8,128)(2,1)S(1)} %get-tuple-element.61), channel_id=1, source_target_pairs={{0,1},{1,0},{2,3},{3,2},{4,5},{5,4},{6,7},{7,6},{8,9},{9,8},{10,11... | collective-permute-start | bytes 61448 | tf_op jit(solution)/shard_map/ppermute | solution.py:362

commit v3 on v2

v3 whole, which is shorter than its diff:
```python
import jax
import jax.numpy as jnp
from jax import lax
from jax.experimental import pallas as pl
from jax.experimental.pallas import tpu as pltpu
from jax.sharding import PartitionSpec as P

SPAN = 4
SOFTMAX_SCALE = 192.0 ** (-0.5)
BLK = 64
RUN = 16
WIDE = 640


def permute(value, to):
    seqs, heads = lax.axis_size("seq"), lax.axis_size("head")
    pairs = []
    for i in range(seqs):
        if to(i) is None:
            continue
        j = to(i) % seqs
        for h in range(heads):
            pairs.append((i * heads + h, j * heads + (h ^ 1 if i // RUN != j // RUN else h)))
    return lax.ppermute(value, ("seq", "head"), pairs)


def shift(value, by):
    return permute(value, lambda i: i + by)


def swap_cores(value):
    return permute(value, lambda i: i ^ 1)


def nt(a, b):
    return lax.dot_general(a, b, (((1,), (1,)), ((), ())), preferred_element_type=jnp.float32)


def nn(a, b):
    return lax.dot_general(a, b, (((1,), (0,)), ((), ())), preferred_element_type=jnp.float32)


def tn(a, b):
    return lax.dot_general(a, b, (((0,), (0,)), ((), ())), preferred_element_type=jnp.float32)


def rope_of(packed):
    wide = jnp.concatenate([packed[:, 128 * b : 128 * (b + 1)] for b in range(4)], axis=0)
    return wide.astype(jnp.float32).T.astype(jnp.bfloat16)


def gather_keys(order_ref, me, shards_in_order, refs, bases, rope_ref):
    seqs = order_ref.shape[0] // 2
    low, high = [], []
    for place, s in enumerate(shards_in_order):
        other = lax.rem(me + seqs - s, seqs)
        first, second = order_ref[2 * other], order_ref[2 * other + 1]
        low_slot = jnp.where(first < second, 0, 1)
        at_low = pl.multiple_of(low_slot * BLK, BLK)
        at_high = pl.multiple_of((1 - low_slot) * BLK, BLK)
        rope_ref[place] = rope_of(refs[place][pl.ds(bases[place] + 2 * BLK, 16), :])
        for out, at, pos in ((low, at_low, jnp.minimum(first, second)), (high, at_high, jnp.maximum(first, second))):
            out.append((refs[place][pl.ds(pl.multiple_of(bases[place] + at, 16), BLK), :], rope_ref[place, pl.ds(at, BLK), :], pos, at))
    both = low + high
    keys = jnp.concatenate([x[0] for x in both], axis=0)
    ropes = jnp.concatenate([x[1] for x in both], axis=0)
    return keys, ropes, [x[2] for x in both], [x[3] for x in both]


def own_place(order_ref, me, rows):
    first, second = order_ref[2 * me], order_ref[2 * me + 1]
    high = jnp.where(first > second, 0, 1)
    upper = pl.multiple_of(high * rows, rows)
    lower = pl.multiple_of((1 - high) * rows, rows)
    return jnp.minimum(first, second), jnp.maximum(first, second), lower, upper


def tile(keys, ropes, key_blocks, row_block, q, qr, do, total, dots):
    rows = q.shape[0]
    scores = SOFTMAX_SCALE * (nt(keys, q) + nt(ropes, qr))
    probs = jnp.exp(scores - total)
    ahead = (
        lax.broadcasted_iota(jnp.int32, (BLK, rows), 1) // (rows // BLK)
        - lax.broadcasted_iota(jnp.int32, (BLK, rows), 0)
    )
    pieces = []
    for n, key_block in enumerate(key_blocks):
        piece = probs[n * BLK : (n + 1) * BLK]
        if key_block is not None:
            piece = jnp.where(ahead >= (key_block - row_block) * BLK, piece, 0.0)
        pieces.append(piece)
    probs = jnp.concatenate(pieces, axis=0)
    dprobs = nt(keys, do)
    dscores = (SOFTMAX_SCALE * probs * (dprobs - dots)).astype(jnp.bfloat16)
    return probs.astype(jnp.bfloat16), dscores


def pack_kernel(lat_hbm, rope_hbm, order_hbm, dot_hbm, tot_hbm, own_ref, order_ref, dot_ref, tot_ref, sems):
    pairs = [(lat_hbm, own_ref.at[pl.ds(0, 128), :])]
    for b in range(4):
        pairs.append((rope_hbm.at[pl.ds(16 * b, 16), :], own_ref.at[pl.ds(128, 16), pl.ds(128 * b, 128)]))
    pairs += [(order_hbm, order_ref), (dot_hbm, dot_ref), (tot_hbm, tot_ref)]
    copies = [pltpu.make_async_copy(pair[0], pair[1], sems.at[n]) for n, pair in enumerate(pairs)]
    for copy in copies:
        copy.start()
    for copy in copies:
        copy.wait()


def spread(values):
    heads, tokens = values.shape
    rows = heads * tokens
    pieces, rest = [], values
    for _ in range(3):
        piece = rest.astype(jnp.bfloat16)
        rest = rest - piece.astype(jnp.float32)
        pieces.append(piece)
    column = lax.broadcasted_iota(jnp.int32, (tokens, rows), 1)
    token = lax.broadcasted_iota(jnp.int32, (tokens, rows), 0)
    pick = jnp.where(column // heads == token, 1.0, 0.0).astype(jnp.bfloat16)
    wide = (nn(pieces[0], pick) + nn(pieces[1], pick)) + nn(pieces[2], pick)
    column = lax.broadcasted_iota(jnp.int32, (heads, rows), 1)
    head = lax.broadcasted_iota(jnp.int32, (heads, rows), 0)
    return jnp.sum(jnp.where(lax.rem(column, heads) == head, wide, 0.0), axis=0, keepdims=True)


def window_part(order_ref, me, shards, refs, rope_ref, q_ref, qr_ref, do_ref, dot_ref, tot_ref, outs):
    ds_up_ref, ds_low_ref, keys_ref, ropes_ref = outs
    rows = q_ref.shape[0] // 2
    low_mine, high_mine, lower, upper = own_place(order_ref, me, rows)
    keys, ropes, blocks, at = gather_keys(order_ref, me, shards, refs, (0, 0), rope_ref)
    keys_ref[...] = keys
    ropes_ref[...] = ropes

    def grads(part, key_rows, row_block, seen, ds_ref):
        q, qr, do = q_ref[part, :], qr_ref[part, :], do_ref[part, :]
        probs, ds = tile(
            keys[:key_rows], ropes[:key_rows], seen, row_block, q, qr, do, tot_ref[:, part], dot_ref[:, part]
        )
        ds_ref[...] = ds
        return nn(ds, q) + nn(probs, do), nn(ds, qr)

    lat, grope = grads(pl.ds(upper, rows), 4 * BLK, high_mine, [None, None] + blocks[2:], ds_up_ref)
    lat_low, grope_low = grads(pl.ds(lower, rows), 2 * BLK, low_mine, blocks[:2], ds_low_ref)
    blank = jnp.zeros((BLK, WIDE - 512 - 64), jnp.float32)
    found = []
    for n in range(4):
        cut = slice(n * BLK, (n + 1) * BLK)
        lat_n, grope_n = lat[cut], grope[cut]
        if n < 2:
            lat_n, grope_n = lat_n + lat_low[cut], grope_n + grope_low[cut]
        found.append((at[n], jnp.concatenate([lat_n, grope_n, blank], axis=1)))
    return (found[0], found[2]), (found[1], found[3])


def early_kernel(
    order_ref, own_ref, near_ref, q_ref, qr_ref, do_ref, dot_in, tot_in,
    keep_ref, out_ref, ds_up_ref, ds_low_ref, keys_ref, ropes_ref, dot_ref, tot_ref,
    rope_ref,
):
    me = lax.axis_index("seq")
    dot_ref[...] = spread(dot_in[...])
    tot_ref[...] = spread(tot_in[...])
    shards = (0, jnp.where(lax.rem(me, 2) == 0, 3, 1))
    found = window_part(
        order_ref, me, shards, (own_ref, near_ref), rope_ref, q_ref, qr_ref, do_ref, dot_ref, tot_ref,
        (ds_up_ref, ds_low_ref, keys_ref, ropes_ref),
    )
    for at, value in found[0]:
        keep_ref[pl.ds(at, BLK), :] = value
    for at, value in found[1]:
        out_ref[pl.ds(at, BLK), :] = value.astype(jnp.bfloat16)


def late_kernel(
    order_ref, two_ref, last_ref, q_ref, qr_ref, do_ref, dot_ref, tot_ref,
    keep_ref, out_ref, ds_up_ref, ds_low_ref, keys_ref, ropes_ref,
    rope_ref,
):
    me = lax.axis_index("seq")
    shards = (2, jnp.where(lax.rem(me, 2) == 0, 1, 3))
    found = window_part(
        order_ref, me, shards, (two_ref, last_ref), rope_ref, q_ref, qr_ref, do_ref, dot_ref, tot_ref,
        (ds_up_ref, ds_low_ref, keys_ref, ropes_ref),
    )
    for at, value in found[0]:
        keep_ref[pl.ds(at, BLK), :] = value
    for at, value in found[1]:
        out_ref[pl.ds(at, BLK), :] = value.astype(jnp.bfloat16)


def query_kernel(
    order_ref, up_a_ref, low_a_ref, keys_a_ref, ropes_a_ref, up_b_ref, low_b_ref, keys_b_ref, ropes_b_ref,
    gq_ref, gqr_ref,
):
    me = lax.axis_index("seq")
    rows = up_a_ref.shape[1]
    _, _, lower, upper = own_place(order_ref, me, rows)
    half = 2 * BLK
    for at, a_ref, b_ref, n in ((upper, up_a_ref, up_b_ref, 2 * half), (lower, low_a_ref, low_b_ref, half)):
        part = pl.ds(at, rows)
        ds = jnp.concatenate([a_ref[...], b_ref[...]], axis=0)
        keys = jnp.concatenate([keys_a_ref[:n], keys_b_ref[:n]], axis=0)
        ropes = jnp.concatenate([ropes_a_ref[:n], ropes_b_ref[:n]], axis=0)
        gq_ref[part, :] = tn(ds, keys).astype(jnp.bfloat16)
        gqr_ref[part, :] = tn(ds, ropes).astype(jnp.bfloat16)


VMEM = pl.BlockSpec(memory_space=pltpu.VMEM)
SMEM = pl.BlockSpec(memory_space=pltpu.SMEM)
HBM = pl.BlockSpec(memory_space=pltpu.HBM)


def in_hbm(value):
    return pltpu.with_memory_space_constraint(value, pltpu.HBM)


def call(kernel, args, in_specs, outs, scratch, gflop, aliases={}):
    return pl.pallas_call(
        kernel,
        out_shape=tuple(jax.ShapeDtypeStruct(shape, dtype) for shape, dtype in outs),
        in_specs=in_specs,
        out_specs=(VMEM,) * len(outs),
        scratch_shapes=scratch,
        input_output_aliases=aliases,
        compiler_params=pltpu.CompilerParams(vmem_limit_bytes=32 * 2**20),
        cost_estimate=pl.CostEstimate(
            flops=int(gflop * 1e9), bytes_accessed=int(gflop * 2e6), transcendentals=int(gflop * 1e5)
        ),
    )(*args)


def first_join_kernel(keep_ref, two_ref, early_ref, home_ref, back_ref):
    even = lax.rem(lax.axis_index("seq"), 2) == 0
    early = early_ref[...].astype(jnp.float32)
    home_ref[...] = (keep_ref[...] + jnp.where(even, early, 0.0)).astype(jnp.bfloat16)
    back_ref[...] = two_ref[...] + jnp.where(even, 0.0, early)


def join_kernel(home_ref, back_ref, late_ref, out_ref):
    back = back_ref[...] + late_ref[...].astype(jnp.float32)
    rows = home_ref.shape[0] // 4
    for y in range(4):
        cut = slice(y * rows, (y + 1) * rows)
        out_ref[pl.ds(2 * y * rows, rows), :] = home_ref[cut]
        out_ref[pl.ds((2 * y + 1) * rows, rows), :] = back[cut].astype(jnp.bfloat16)


def y_kernel(parts_ref, keep_ref, send_ref):
    whole = parts_ref[0].astype(jnp.float32)
    for n in range(1, parts_ref.shape[0]):
        whole = whole + parts_ref[n].astype(jnp.float32)
    rows = keep_ref.shape[0]
    keep_ref[...] = whole[:rows]
    send_ref[...] = whole[rows:].astype(jnp.bfloat16)


def share_kernel(mine_ref, got_ref, keep_ref, send_ref):
    whole = mine_ref[...] + got_ref[...].astype(jnp.float32)
    rows = keep_ref.shape[0]
    first = lax.rem(lax.axis_index("head"), 2) == 0
    keep_ref[...] = jnp.where(first, whole[:rows], whole[rows:])
    send_ref[...] = jnp.where(first, whole[rows:], whole[:rows]).astype(jnp.bfloat16)


def last_kernel(keep_ref, got_ref, lat_ref, rope_ref):
    whole = keep_ref[...] + got_ref[...].astype(jnp.float32)
    lat_ref[...] = whole[:, :512].astype(jnp.bfloat16)
    rope_ref[...] = whole[:, 512:576].astype(jnp.bfloat16)


def shards(q_lat, q_rope, d_out, latent, key_rope, forward_dot, log_total, block_order):
    tokens, heads, width = q_lat.shape
    rows = tokens * heads
    half, bf16, f32 = rows // 2, jnp.bfloat16, jnp.float32
    own, order, dots, sums = call(
        pack_kernel,
        tuple(in_hbm(x) for x in (latent, key_rope, block_order, forward_dot, log_total)),
        [HBM] * 5,
        [
            ((tokens + 16, width), bf16),
            (block_order.shape, jnp.int32),
            (forward_dot.shape, f32),
            (log_total.shape, f32),
        ],
        [pltpu.SemaphoreType.DMA((8,))],
        20.0,
    )
    first = permute(own, lambda i: i + 3 if i % 2 else i + 1)
    two_back = shift(own, 2)
    last = permute(own, lambda i: i + 1 if i % 2 else i + 3)
    q, qr, do = q_lat.reshape(rows, width), q_rope.reshape(rows, 64), d_out.reshape(rows, width)
    kept = [((256, half), bf16), ((128, half), bf16), ((256, width), bf16), ((256, 64), bf16)]
    whole, vector = ((rows, width), bf16), ((1, rows), f32)
    keep, far, up_a, low_a, keys_a, ropes_a, dots, sums = call(
        early_kernel,
        (
            order, own, first, q, qr, do, dots, sums,
        ),
        [SMEM] + [VMEM] * 7,
        [((tokens, WIDE), f32), ((tokens, WIDE), bf16)] + kept + [vector, vector],
        [pltpu.VMEM((2, 128, 64), bf16)],
        0.0,
    )
    early_sent = shift(far, -1)
    two, other, up_b, low_b, keys_b, ropes_b = call(
        late_kernel,
        (order, two_back, last, q, qr, do, dots, sums),
        [SMEM] + [VMEM] * 7,
        [((tokens, WIDE), f32), ((tokens, WIDE), bf16)] + kept,
        [pltpu.VMEM((2, 128, 64), bf16)],
        0.0,
    )
    late_sent = swap_cores(other)
    grad_q, grad_qr = call(
        query_kernel,
        (order, up_a, low_a, keys_a, ropes_a, up_b, low_b, keys_b, ropes_b),
        [SMEM] + [VMEM] * 8,
        [whole, ((rows, 64), bf16)],
        [],
        0.05,
    )
    grad_qr = grad_qr.reshape(tokens, heads * 64)
    home, back = call(
        first_join_kernel,
        (keep, two, early_sent),
        [VMEM] * 3,
        [((tokens, WIDE), bf16), ((tokens, WIDE), f32)],
        [],
        0.0,
    )
    (joined,) = call(join_kernel, (home, back, late_sent), [VMEM] * 3, [((2 * tokens, WIDE), bf16)], [], 0.0)
    parts = lax.all_to_all(
        joined, "head", 0, 0, tiled=True, axis_index_groups=[[0, 2, 4, 6], [1, 3, 5, 7]]
    ).reshape(4, tokens // 2, WIDE)
    quarter, share = tokens // 4, tokens // 8
    mine, passed = call(
        y_kernel, (parts,), [VMEM], [((quarter, WIDE), f32), ((quarter, WIDE), bf16)], [], 0.0
    )
    kept, given = call(
        share_kernel,
        (mine, shift(passed, -2)),
        [VMEM] * 2,
        [((share, WIDE), f32), ((share, WIDE), bf16)],
        [],
        0.0,
    )
    got = lax.ppermute(given, "head", [(h, h ^ 1) for h in range(8)])
    lat_grad, rope_grad = call(
        last_kernel, (kept, got), [VMEM] * 2, [((share, width), bf16), ((share, 64), bf16)], [], 0.0
    )
    return grad_q.reshape(tokens, heads, width), grad_qr, lat_grad, rope_grad


def solution(mesh):
    return jax.shard_map(
        shards,
        mesh=mesh,
        in_specs=(
            P("seq", "head", None),
            P("seq", "head"),
            P("seq", "head", None),
            P("seq", None),
            P(None, "seq"),
            P("head", "seq"),
            P("head", "seq"),
            P(),
        ),
        out_specs=(
            P("seq", "head", None),
            P("seq", "head"),
            P(("seq", "head"), None),
            P(("seq", "head"), None),
        ),
        check_vma=False,
    )
```

time: 70.7 us -> 63.3 us (0.90)
  the two profiles are of different devices: /device:TPU:1 before, /device:TPU:8 now
where the time goes in v3:
time: 63.3 us; the launch traced here: 62.9 us
  starting transfers between devices  32.4 us (51%)
  blocking collectives  10.9 us (17%)
  waiting for transfers between devices  9.21 us (15%)
  Pallas kernels  8.56 us (14%)
  local copies, waits for them, and re-layouts  1.06 us (2%)
  between operations  0.79 us (1%)
    ppermute x6, starting transfers between devices, permute(): return lax.ppermute(value, ('seq', 'head'), pairs)  22.3 us
    all_to_all x1, blocking collectives, shards(): lax.all_to_all(joined, 'head', 0, 0, tiled=True, axis_index_groups=[[0, 2...  10.9 us
    ppermute x1, starting transfers between devices, shards(): got = lax.ppermute(given, 'head', [(h, h ^ 1) for h in range(8)])  10.1 us
    pallas_call x9, Pallas kernels, call(): pl.pallas_call(kernel, out_shape=tuple((jax.ShapeDtypeStruct(shape, dtype...  8.56 us
    ppermute x6, waiting for transfers between devices, permute(): return lax.ppermute(value, ('seq', 'head'), pairs)  8.09 us
  transfers between devices with their start and end apart: 7, of which 5 were waited for; matrix products, arithmetic and copies ran while one was open for 2% of the time, Pallas kernels for 11%

profile of v3, /device:TPU:8, one launch (start us, length us, event | category | flops | bytes accessed | tf_op | source)
XLA Modules:
  0.0 62.9 jit_solution(9905878117048325563)
XLA Ops:
  0.6 0.0 copy-start.2
  0.6 0.0 copy-start
  0.7 0.0 copy-start.1
  0.7 1.1 %shard_map.111 = (bf16[144,512]{1,0:T(8,128)(2,1)S(1)}, s32[128]{0:T(128)S(1)}, f32[8,128]{1,0:T(8,128)S(1)}, f32[8,128]{1,0:T(8,128)S(1)}) custom-call(bf16[128,512]{1,0:T(8,128)(2,1)} %lat_hbm.1, bf16[64,128]{1,0:T(8,128)(2,1)} %rope_hbm.1, s32[128]{0:T(128)} %order_hbm.1, f32[8,128]{1,0:T(8,128)} %dot_hbm.1, f32[8,128]{1,0:T(8,128)} %tot_hbm.1), custom_call_target="tpu_custom_call" | custom-call | flops 20000000000 | bytes 40000000 | tf_op jit(solution)/shard_map/pallas_call | solution.py:219
  1.8 1.9 %collective-permute-start = (bf16[144,512]{1,0:T(8,128)(2,1)S(1)}, bf16[144,512]{1,0:T(8,128)(2,1)S(1)}, u32[]{:S(2)}, u32[]{:S(2)}) collective-permute-start(bf16[144,512]{1,0:T(8,128)(2,1)S(1)} %get-tuple-element.33.own_ref), channel_id=1, source_target_pairs={{0,8},{1,9},{2,10},{3,11},{4,12},{5,13},{6,14},{7,15},{8,32},{9,33... | collective-permute-start | bytes 442376 | tf_op jit(solution)/shard_map/ppermute | solution.py:24
  3.7 3.8 %collective-permute-start.1 = (bf16[144,512]{1,0:T(8,128)(2,1)S(1)}, bf16[144,512]{1,0:T(8,128)(2,1)S(1)}, u32[]{:S(2)}, u32[]{:S(2)}) collective-permute-start(bf16[144,512]{1,0:T(8,128)(2,1)S(1)} %get-tuple-element.33.own_ref), channel_id=1, source_target_pairs={{0,16},{1,17},{2,18},{3,19},{4,20},{5,21},{6,22},{7,23},{8,24},{9,... | collective-permute-start | bytes 442376 | tf_op jit(solution)/shard_map/ppermute | solution.py:24
  7.6 7.7 %collective-permute-start.2 = (bf16[144,512]{1,0:T(8,128)(2,1)S(1)}, bf16[144,512]{1,0:T(8,128)(2,1)S(1)}, u32[]{:S(2)}, u32[]{:S(2)}) collective-permute-start(bf16[144,512]{1,0:T(8,128)(2,1)S(1)} %get-tuple-element.33.own_ref), channel_id=1, source_target_pairs={{0,24},{1,25},{2,26},{3,27},{4,28},{5,29},{6,30},{7,31},{8,16},{9,... | collective-permute-start | bytes 442376 | tf_op jit(solution)/shard_map/ppermute | solution.py:24
  15.3 0.0 copy-done.2
  15.3 0.2 reshape.28.qr_ref
  15.5 2.7 %collective-permute-done.near_ref = bf16[144,512]{1,0:T(8,128)(2,1)S(1)} collective-permute-done((bf16[144,512]{1,0:T(8,128)(2,1)S(1)}, bf16[144,512]{1,0:T(8,128)(2,1)S(1)}, u32[]{:S(2)}, u32[]{:S(2)}) %collective-permute-start) | collective-permute-done | bytes 147488 | tf_op jit(solution)/shard_map/ppermute | solution.py:24
  18.2 0.0 copy-done
  18.2 0.0 copy-done.1
  18.2 2.2 %shard_map.112 = (f32[128,640]{1,0:T(8,128)S(1)}, bf16[128,640]{1,0:T(8,128)(2,1)S(1)}, bf16[256,512]{1,0:T(8,128)(2,1)S(1)}, bf16[128,512]{1,0:T(8,128)(2,1)S(1...) custom-call(s32[128]{0:T(128)S(1)} %get-tuple-element.32.order_ref, ...), custom_call_target="tpu_custom_call" | custom-call | tf_op jit(solution)/shard_map/pallas_call | solution.py:219
  20.4 2.6 %collective-permute-start.3 = (bf16[128,640]{1,0:T(8,128)(2,1)S(1)}, bf16[128,640]{1,0:T(8,128)(2,1)S(1)}, u32[]{:S(2)}, u32[]{:S(2)}) collective-permute-start(bf16[128,640]{1,0:T(8,128)(2,1)S(1)} %get-tuple-element.50), channel_id=1, source_target_pairs={{0,505},{1,504},{2,507},{3,506},{4,509},{5,508},{6,511},{7,510},{8... | collective-permute-start | bytes 491528 | tf_op jit(solution)/shard_map/ppermute | solution.py:24
  23.1 0.0 collective-permute-done.1.two_ref
  23.1 2.5 %collective-permute-done.2.last_ref = bf16[144,512]{1,0:T(8,128)(2,1)S(1)} collective-permute-done((bf16[144,512]{1,0:T(8,128)(2,1)S(1)}, bf16[144,512]{1,0:T(8,128)(2,1)S(1)}, u32[]{:S(2)}, u32[]{:S(2)}) %collective-permute-start.2) | collective-permute-done | bytes 147488 | tf_op jit(solution)/shard_map/ppermute | solution.py:24
  25.6 2.1 %shard_map.113 = (f32[128,640]{1,0:T(8,128)S(1)}, bf16[128,640]{1,0:T(8,128)(2,1)S(1)}, bf16[256,512]{1,0:T(8,128)(2,1)S(1)}, bf16[128,512]{1,0:T(8,128)(2,1)S(1...) custom-call(s32[128]{0:T(128)S(1)} %get-tuple-element.32.order_ref, ...), custom_call_target="tpu_custom_call" | custom-call | tf_op jit(solution)/shard_map/pallas_call | solution.py:219
  27.7 1.9 %collective-permute-start.4 = (bf16[128,640]{1,0:T(8,128)(2,1)S(1)}, bf16[128,640]{1,0:T(8,128)(2,1)S(1)}, u32[]{:S(2)}, u32[]{:S(2)}) collective-permute-start(bf16[128,640]{1,0:T(8,128)(2,1)S(1)} %get-tuple-element.53), channel_id=1, source_target_pairs={{0,8},{1,9},{2,10},{3,11},{4,12},{5,13},{6,14},{7,15},{8,0},{9,1},... | collective-permute-start | bytes 491528 | tf_op jit(solution)/shard_map/ppermute | solution.py:24
  29.6 0.0 collective-permute-done.3.early_ref
  29.6 0.1 shard_map.115
  29.7 1.3 %collective-permute-done.4.late_ref = bf16[128,640]{1,0:T(8,128)(2,1)S(1)} collective-permute-done((bf16[128,640]{1,0:T(8,128)(2,1)S(1)}, bf16[128,640]{1,0:T(8,128)(2,1)S(1)}, u32[]{:S(2)}, u32[]{:S(2)}) %collective-permute-start.4) | collective-permute-done | bytes 163872 | tf_op jit(solution)/shard_map/ppermute | solution.py:24
  31.0 0.1 shard_map.116
  31.0 10.9 %all_to_all.9.parts_ref = bf16[4,64,640]{2,1,0:T(8,128)(2,1)S(1)} all-to-all(bf16[4,64,640]{2,1,0:T(8,128)(2,1)S(1)} %bitcast.8), channel_id=1, replica_groups={{0,2,4,6},{1,3,5,7},{8,10,12,14},{9,11,13,15},{16,18,20,22},{17,19,21,2..., dimensions={0} | all-to-all | bytes 655360 | tf_op jit(solution)/shard_map/all_to_all | solution.py:333
  42.0 4.3 %collective-permute-start.5 = (bf16[32,640]{1,0:T(8,128)(2,1)S(1)}, bf16[32,640]{1,0:T(8,128)(2,1)S(1)}, u32[]{:S(2)}, u32[]{:S(2)}) collective-permute-start(bf16[32,640]{1,0:T(8,128)(2,1)S(1)} %get-tuple-element.55), channel_id=1, source_target_pairs={{0,497},{1,496},{2,499},{3,498},{4,501},{5,500},{6,503},{7,502},{8... | collective-permute-start | bytes 122888 | tf_op jit(solution)/shard_map/ppermute | solution.py:24
  46.3 1.7 %collective-permute-done.5.got_ref = bf16[32,640]{1,0:T(8,128)(2,1)S(1)} collective-permute-done((bf16[32,640]{1,0:T(8,128)(2,1)S(1)}, bf16[32,640]{1,0:T(8,128)(2,1)S(1)}, u32[]{:S(2)}, u32[]{:S(2)}) %collective-permute-start.5) | collective-permute-done | bytes 40992 | tf_op jit(solution)/shard_map/ppermute | solution.py:24
  47.9 10.1 %collective-permute-start.6 = (bf16[16,640]{1,0:T(8,128)(2,1)S(1)}, bf16[16,640]{1,0:T(8,128)(2,1)S(1)}, u32[]{:S(2)}, u32[]{:S(2)}) collective-permute-start(bf16[16,640]{1,0:T(8,128)(2,1)S(1)} %get-tuple-element.57), channel_id=1, source_target_pairs={{0,1},{1,0},{2,3},{3,2},{4,5},{5,4},{6,7},{7,6},{8,9},{9,8},{10,11... | collective-permute-start | bytes 61448 | tf_op jit(solution)/shard_map/ppermute | solution.py:348
  58.0 2.3 %shard_map.114 = (bf16[1024,512]{1,0:T(8,128)(2,1)}, bf16[1024,64]{1,0:T(8,128)(2,1)S(1)}) custom-call(s32[128]{0:T(128)S(1)} %get-tuple-element.32.order_ref, bf16[256,512]{1,0:T(8,128)(2,1)S(1)} %get-tuple-element.36.up_a_ref, bf16[128,512]{1,0:T(8,128)(2,1)S(1)} %get-tuple-element.37.low_a_ref, bf16[256,512]{1,0:T(8,128)(2,1)S(1)} %get-tuple-element.38.keys_a_ref, ...), custom_call_target="tpu_custom_call" | custom-call | flops 50000000 | bytes 100000 | tf_op jit(solution)/shard_map/pallas_call | solution.py:219
  60.3 0.9 %reshape.31 = bf16[128,512]{1,0:T(8,128)(2,1)} reshape(bf16[1024,64]{1,0:T(8,128)(2,1)S(1)} %get-tuple-element.47) | data formatting | bytes 262144 | tf_op jit(solution)/shard_map/reshape | solution.py:323
  61.2 1.1 %collective-permute-done.6.got_ref = bf16[16,640]{1,0:T(8,128)(2,1)S(1)} collective-permute-done((bf16[16,640]{1,0:T(8,128)(2,1)S(1)}, bf16[16,640]{1,0:T(8,128)(2,1)S(1)}, u32[]{:S(2)}, u32[]{:S(2)}) %collective-permute-start.6) | collective-permute-done | bytes 20512 | tf_op jit(solution)/shard_map/ppermute | solution.py:348
  62.3 0.6 shard_map.119
  (2 shorter events, 0.1 us)
Async XLA Ops:
  0.6 14.7 %copy-start.2 = (bf16[128,512]{1,0:T(8,128)(2,1)S(1)}, bf16[128,512]{1,0:T(8,128)(2,1)}, u32[]{:S(2)}) copy-start(bf16[128,512]{1,0:T(8,128)(2,1)} %param.9) | copy-start | bytes 393220
  0.6 17.6 %copy-start = (bf16[128,8,512]{2,1,0:T(8,128)(2,1)S(1)}, bf16[128,8,512]{2,1,0:T(8,128)(2,1)}, u32[]{:S(2)}) copy-start(bf16[128,8,512]{2,1,0:T(8,128)(2,1)} %param.8) | copy-start | bytes 3145732
  0.7 17.6 %copy-start.1 = (bf16[128,8,512]{2,1,0:T(8,128)(2,1)S(1)}, bf16[128,8,512]{2,1,0:T(8,128)(2,1)}, u32[]{:S(2)}) copy-start(bf16[128,8,512]{2,1,0:T(8,128)(2,1)} %param.10) | copy-start | bytes 3145732
  1.8 16.4 %collective-permute-start = (bf16[144,512]{1,0:T(8,128)(2,1)S(1)}, bf16[144,512]{1,0:T(8,128)(2,1)S(1)}, u32[]{:S(2)}, u32[]{:S(2)}) collective-permute-start(bf16[144,512]{1,0:T(8,128)(2,1)S(1)} %get-tuple-element.33.own_ref), channel_id=1, source_target_pairs={{0,8},{1,9},{2,10},{3,11},{4,12},{5,13},{6,14},{7,15},{8,32},{9,33... | collective-permute-start | bytes 442376 | tf_op jit(solution)/shard_map/ppermute | solution.py:24
  3.7 19.3 %collective-permute-start.1 = (bf16[144,512]{1,0:T(8,128)(2,1)S(1)}, bf16[144,512]{1,0:T(8,128)(2,1)S(1)}, u32[]{:S(2)}, u32[]{:S(2)}) collective-permute-start(bf16[144,512]{1,0:T(8,128)(2,1)S(1)} %get-tuple-element.33.own_ref), channel_id=1, source_target_pairs={{0,16},{1,17},{2,18},{3,19},{4,20},{5,21},{6,22},{7,23},{8,24},{9,... | collective-permute-start | bytes 442376 | tf_op jit(solution)/shard_map/ppermute | solution.py:24
  7.6 18.0 %collective-permute-start.2 = (bf16[144,512]{1,0:T(8,128)(2,1)S(1)}, bf16[144,512]{1,0:T(8,128)(2,1)S(1)}, u32[]{:S(2)}, u32[]{:S(2)}) collective-permute-start(bf16[144,512]{1,0:T(8,128)(2,1)S(1)} %get-tuple-element.33.own_ref), channel_id=1, source_target_pairs={{0,24},{1,25},{2,26},{3,27},{4,28},{5,29},{6,30},{7,31},{8,16},{9,... | collective-permute-start | bytes 442376 | tf_op jit(solution)/shard_map/ppermute | solution.py:24
  20.4 9.2 %collective-permute-start.3 = (bf16[128,640]{1,0:T(8,128)(2,1)S(1)}, bf16[128,640]{1,0:T(8,128)(2,1)S(1)}, u32[]{:S(2)}, u32[]{:S(2)}) collective-permute-start(bf16[128,640]{1,0:T(8,128)(2,1)S(1)} %get-tuple-element.50), channel_id=1, source_target_pairs={{0,505},{1,504},{2,507},{3,506},{4,509},{5,508},{6,511},{7,510},{8... | collective-permute-start | bytes 491528 | tf_op jit(solution)/shard_map/ppermute | solution.py:24
  27.7 3.3 %collective-permute-start.4 = (bf16[128,640]{1,0:T(8,128)(2,1)S(1)}, bf16[128,640]{1,0:T(8,128)(2,1)S(1)}, u32[]{:S(2)}, u32[]{:S(2)}) collective-permute-start(bf16[128,640]{1,0:T(8,128)(2,1)S(1)} %get-tuple-element.53), channel_id=1, source_target_pairs={{0,8},{1,9},{2,10},{3,11},{4,12},{5,13},{6,14},{7,15},{8,0},{9,1},... | collective-permute-start | bytes 491528 | tf_op jit(solution)/shard_map/ppermute | solution.py:24
  42.0 5.9 %collective-permute-start.5 = (bf16[32,640]{1,0:T(8,128)(2,1)S(1)}, bf16[32,640]{1,0:T(8,128)(2,1)S(1)}, u32[]{:S(2)}, u32[]{:S(2)}) collective-permute-start(bf16[32,640]{1,0:T(8,128)(2,1)S(1)} %get-tuple-element.55), channel_id=1, source_target_pairs={{0,497},{1,496},{2,499},{3,498},{4,501},{5,500},{6,503},{7,502},{8... | collective-permute-start | bytes 122888 | tf_op jit(solution)/shard_map/ppermute | solution.py:24
  47.9 14.4 %collective-permute-start.6 = (bf16[16,640]{1,0:T(8,128)(2,1)S(1)}, bf16[16,640]{1,0:T(8,128)(2,1)S(1)}, u32[]{:S(2)}, u32[]{:S(2)}) collective-permute-start(bf16[16,640]{1,0:T(8,128)(2,1)S(1)} %get-tuple-element.57), channel_id=1, source_target_pairs={{0,1},{1,0},{2,3},{3,2},{4,5},{5,4},{6,7},{7,6},{8,9},{9,8},{10,11... | collective-permute-start | bytes 61448 | tf_op jit(solution)/shard_map/ppermute | solution.py:348

commit v4 on v3

--- a/solution.py
+++ b/solution.py
@@ -239,20 +239,21 @@
 
 def join_kernel(home_ref, back_ref, late_ref, out_ref):
     back = back_ref[...] + late_ref[...].astype(jnp.float32)
-    rows = home_ref.shape[0] // 4
-    for y in range(4):
-        cut = slice(y * rows, (y + 1) * rows)
-        out_ref[pl.ds(2 * y * rows, rows), :] = home_ref[cut]
-        out_ref[pl.ds((2 * y + 1) * rows, rows), :] = back[cut].astype(jnp.bfloat16)
+    out_ref[:, :512] = home_ref[:, :512]
+    out_ref[:, 512:1024] = back[:, :512].astype(jnp.bfloat16)
+    ropes = jnp.concatenate([home_ref[:, 512:576].astype(jnp.float32), back[:, 512:576]], axis=1)
+    out_ref[:, 1024:] = ropes.astype(jnp.bfloat16)
 
 
 def y_kernel(parts_ref, keep_ref, send_ref):
     whole = parts_ref[0].astype(jnp.float32)
     for n in range(1, parts_ref.shape[0]):
         whole = whole + parts_ref[n].astype(jnp.float32)
-    rows = keep_ref.shape[0]
-    keep_ref[...] = whole[:rows]
-    send_ref[...] = whole[rows:].astype(jnp.bfloat16)
+    ropes = whole[:, 1024:]
+    keep_ref[:, :512] = whole[:, :512]
+    keep_ref[:, 512:] = ropes
+    send_ref[:, :512] = whole[:, 512:1024].astype(jnp.bfloat16)
+    send_ref[:, 512:] = jnp.concatenate([ropes[:, 64:], ropes[:, :64]], axis=1).astype(jnp.bfloat16)
 
 
 def share_kernel(mine_ref, got_ref, keep_ref, send_ref):
@@ -329,10 +330,10 @@
         [],
         0.0,
     )
-    (joined,) = call(join_kernel, (home, back, late_sent), [VMEM] * 3, [((2 * tokens, WIDE), bf16)], [], 0.0)
+    (joined,) = call(join_kernel, (home, back, late_sent), [VMEM] * 3, [((tokens, 1152), bf16)], [], 0.0)
     parts = lax.all_to_all(
         joined, "head", 0, 0, tiled=True, axis_index_groups=[[0, 2, 4, 6], [1, 3, 5, 7]]
-    ).reshape(4, tokens // 2, WIDE)
+    ).reshape(4, tokens // 4, 1152)
     quarter, share = tokens // 4, tokens // 8
     mine, passed = call(
         y_kernel, (parts,), [VMEM], [((quarter, WIDE), f32), ((quarter, WIDE), bf16)], [], 0.0

time: 63.3 us -> 63 us (level)
  the two profiles are of different devices: /device:TPU:8 before, /device:TPU:1 now
where the time goes in v4:
time: 63 us; the launch traced here: 62.1 us
  starting transfers between devices  35.6 us (57%)
  blocking collectives  10.4 us (17%)
  Pallas kernels  8.67 us (14%)
  waiting for transfers between devices  5.49 us (9%)
  local copies, waits for them, and re-layouts  1.06 us (2%)
  between operations  0.81 us (1%)
    ppermute x6, starting transfers between devices, permute(): return lax.ppermute(value, ('seq', 'head'), pairs)  26.4 us
    all_to_all x1, blocking collectives, shards(): lax.all_to_all(joined, 'head', 0, 0, tiled=True, axis_index_groups=[[0, 2...  10.4 us
    ppermute x1, starting transfers between devices, shards(): got = lax.ppermute(given, 'head', [(h, h ^ 1) for h in range(8)])  9.26 us
    pallas_call x9, Pallas kernels, call(): pl.pallas_call(kernel, out_shape=tuple((jax.ShapeDtypeStruct(shape, dtype...  8.67 us
    ppermute x6, waiting for transfers between devices, permute(): return lax.ppermute(value, ('seq', 'head'), pairs)  4.52 us
  transfers between devices with their start and end apart: 7, of which 4 were waited for; matrix products, arithmetic and copies ran while one was open for 2% of the time, Pallas kernels for 11%

profile of v4, /device:TPU:1, one launch (start us, length us, event | category | flops | bytes accessed | tf_op | source)
XLA Modules:
  0.0 62.1 jit_solution(10050556071915594232)
XLA Ops:
  0.6 0.0 copy-start.2
  0.6 0.0 copy-start
  0.7 0.0 copy-start.1
  0.7 1.1 %shard_map.111 = (bf16[144,512]{1,0:T(8,128)(2,1)S(1)}, s32[128]{0:T(128)S(1)}, f32[8,128]{1,0:T(8,128)S(1)}, f32[8,128]{1,0:T(8,128)S(1)}) custom-call(bf16[128,512]{1,0:T(8,128)(2,1)} %lat_hbm.1, bf16[64,128]{1,0:T(8,128)(2,1)} %rope_hbm.1, s32[128]{0:T(128)} %order_hbm.1, f32[8,128]{1,0:T(8,128)} %dot_hbm.1, f32[8,128]{1,0:T(8,128)} %tot_hbm.1), custom_call_target="tpu_custom_call" | custom-call | flops 20000000000 | bytes 40000000 | tf_op jit(solution)/shard_map/pallas_call | solution.py:219
  1.8 6.3 %collective-permute-start = (bf16[144,512]{1,0:T(8,128)(2,1)S(1)}, bf16[144,512]{1,0:T(8,128)(2,1)S(1)}, u32[]{:S(2)}, u32[]{:S(2)}) collective-permute-start(bf16[144,512]{1,0:T(8,128)(2,1)S(1)} %get-tuple-element.33.own_ref), channel_id=1, source_target_pairs={{0,8},{1,9},{2,10},{3,11},{4,12},{5,13},{6,14},{7,15},{8,32},{9,33... | collective-permute-start | bytes 442376 | tf_op jit(solution)/shard_map/ppermute | solution.py:24
  8.1 3.5 %collective-permute-start.1 = (bf16[144,512]{1,0:T(8,128)(2,1)S(1)}, bf16[144,512]{1,0:T(8,128)(2,1)S(1)}, u32[]{:S(2)}, u32[]{:S(2)}) collective-permute-start(bf16[144,512]{1,0:T(8,128)(2,1)S(1)} %get-tuple-element.33.own_ref), channel_id=1, source_target_pairs={{0,16},{1,17},{2,18},{3,19},{4,20},{5,21},{6,22},{7,23},{8,24},{9,... | collective-permute-start | bytes 442376 | tf_op jit(solution)/shard_map/ppermute | solution.py:24
  11.7 1.9 %collective-permute-start.2 = (bf16[144,512]{1,0:T(8,128)(2,1)S(1)}, bf16[144,512]{1,0:T(8,128)(2,1)S(1)}, u32[]{:S(2)}, u32[]{:S(2)}) collective-permute-start(bf16[144,512]{1,0:T(8,128)(2,1)S(1)} %get-tuple-element.33.own_ref), channel_id=1, source_target_pairs={{0,24},{1,25},{2,26},{3,27},{4,28},{5,29},{6,30},{7,31},{8,16},{9,... | collective-permute-start | bytes 442376 | tf_op jit(solution)/shard_map/ppermute | solution.py:24
  13.6 0.0 copy-done.2
  13.6 0.2 reshape.28.qr_ref
  13.8 0.0 collective-permute-done.near_ref
  13.8 0.0 copy-done
  13.8 0.0 copy-done.1
  13.8 2.2 %shard_map.112 = (f32[128,640]{1,0:T(8,128)S(1)}, bf16[128,640]{1,0:T(8,128)(2,1)S(1)}, bf16[256,512]{1,0:T(8,128)(2,1)S(1)}, bf16[128,512]{1,0:T(8,128)(2,1)S(1...) custom-call(s32[128]{0:T(128)S(1)} %get-tuple-element.32.order_ref, ...), custom_call_target="tpu_custom_call" | custom-call | tf_op jit(solution)/shard_map/pallas_call | solution.py:219
  16.0 7.8 %collective-permute-start.3 = (bf16[128,640]{1,0:T(8,128)(2,1)S(1)}, bf16[128,640]{1,0:T(8,128)(2,1)S(1)}, u32[]{:S(2)}, u32[]{:S(2)}) collective-permute-start(bf16[128,640]{1,0:T(8,128)(2,1)S(1)} %get-tuple-element.50), channel_id=1, source_target_pairs={{0,505},{1,504},{2,507},{3,506},{4,509},{5,508},{6,511},{7,510},{8... | collective-permute-start | bytes 491528 | tf_op jit(solution)/shard_map/ppermute | solution.py:24
  23.8 0.0 collective-permute-done.1.two_ref
  23.8 2.5 %collective-permute-done.2.last_ref = bf16[144,512]{1,0:T(8,128)(2,1)S(1)} collective-permute-done((bf16[144,512]{1,0:T(8,128)(2,1)S(1)}, bf16[144,512]{1,0:T(8,128)(2,1)S(1)}, u32[]{:S(2)}, u32[]{:S(2)}) %collective-permute-start.2) | collective-permute-done | bytes 147488 | tf_op jit(solution)/shard_map/ppermute | solution.py:24
  26.4 2.1 %shard_map.113 = (f32[128,640]{1,0:T(8,128)S(1)}, bf16[128,640]{1,0:T(8,128)(2,1)S(1)}, bf16[256,512]{1,0:T(8,128)(2,1)S(1)}, bf16[128,512]{1,0:T(8,128)(2,1)S(1...) custom-call(s32[128]{0:T(128)S(1)} %get-tuple-element.32.order_ref, ...), custom_call_target="tpu_custom_call" | custom-call | tf_op jit(solution)/shard_map/pallas_call | solution.py:219
  28.5 2.6 %collective-permute-start.4 = (bf16[128,640]{1,0:T(8,128)(2,1)S(1)}, bf16[128,640]{1,0:T(8,128)(2,1)S(1)}, u32[]{:S(2)}, u32[]{:S(2)}) collective-permute-start(bf16[128,640]{1,0:T(8,128)(2,1)S(1)} %get-tuple-element.53), channel_id=1, source_target_pairs={{0,8},{1,9},{2,10},{3,11},{4,12},{5,13},{6,14},{7,15},{8,0},{9,1},... | collective-permute-start | bytes 491528 | tf_op jit(solution)/shard_map/ppermute | solution.py:24
  31.1 0.0 collective-permute-done.3.early_ref
  31.1 0.1 shard_map.115
  31.2 0.9 %collective-permute-done.4.late_ref = bf16[128,640]{1,0:T(8,128)(2,1)S(1)} collective-permute-done((bf16[128,640]{1,0:T(8,128)(2,1)S(1)}, bf16[128,640]{1,0:T(8,128)(2,1)S(1)}, u32[]{:S(2)}, u32[]{:S(2)}) %collective-permute-start.4) | collective-permute-done | bytes 163872 | tf_op jit(solution)/shard_map/ppermute | solution.py:24
  32.1 0.1 shard_map.116
  32.2 10.4 %all_to_all.9.parts_ref = bf16[4,32,1152]{2,1,0:T(8,128)(2,1)S(1)} all-to-all(bf16[4,32,1152]{2,1,0:T(8,128)(2,1)S(1)} %bitcast.8), channel_id=1, replica_groups={{0,2,4,6},{1,3,5,7},{8,10,12,14},{9,11,13,15},{16,18,20,22},{17,19,21,2..., dimensions={0} | all-to-all | bytes 589824 | tf_op jit(solution)/shard_map/all_to_all | solution.py:334
  42.6 0.1 shard_map.117
  42.7 4.2 %collective-permute-start.5 = (bf16[32,640]{1,0:T(8,128)(2,1)S(1)}, bf16[32,640]{1,0:T(8,128)(2,1)S(1)}, u32[]{:S(2)}, u32[]{:S(2)}) collective-permute-start(bf16[32,640]{1,0:T(8,128)(2,1)S(1)} %get-tuple-element.55), channel_id=1, source_target_pairs={{0,497},{1,496},{2,499},{3,498},{4,501},{5,500},{6,503},{7,502},{8... | collective-permute-start | bytes 122888 | tf_op jit(solution)/shard_map/ppermute | solution.py:24
  46.9 1.1 %collective-permute-done.5.got_ref = bf16[32,640]{1,0:T(8,128)(2,1)S(1)} collective-permute-done((bf16[32,640]{1,0:T(8,128)(2,1)S(1)}, bf16[32,640]{1,0:T(8,128)(2,1)S(1)}, u32[]{:S(2)}, u32[]{:S(2)}) %collective-permute-start.5) | collective-permute-done | bytes 40992 | tf_op jit(solution)/shard_map/ppermute | solution.py:24
  48.0 9.3 %collective-permute-start.6 = (bf16[16,640]{1,0:T(8,128)(2,1)S(1)}, bf16[16,640]{1,0:T(8,128)(2,1)S(1)}, u32[]{:S(2)}, u32[]{:S(2)}) collective-permute-start(bf16[16,640]{1,0:T(8,128)(2,1)S(1)} %get-tuple-element.57), channel_id=1, source_target_pairs={{0,1},{1,0},{2,3},{3,2},{4,5},{5,4},{6,7},{7,6},{8,9},{9,8},{10,11... | collective-permute-start | bytes 61448 | tf_op jit(solution)/shard_map/ppermute | solution.py:349
  57.3 2.3 %shard_map.114 = (bf16[1024,512]{1,0:T(8,128)(2,1)}, bf16[1024,64]{1,0:T(8,128)(2,1)S(1)}) custom-call(s32[128]{0:T(128)S(1)} %get-tuple-element.32.order_ref, bf16[256,512]{1,0:T(8,128)(2,1)S(1)} %get-tuple-element.36.up_a_ref, bf16[128,512]{1,0:T(8,128)(2,1)S(1)} %get-tuple-element.37.low_a_ref, bf16[256,512]{1,0:T(8,128)(2,1)S(1)} %get-tuple-element.38.keys_a_ref, ...), custom_call_target="tpu_custom_call" | custom-call | flops 50000000 | bytes 100000 | tf_op jit(solution)/shard_map/pallas_call | solution.py:219
  59.6 0.9 %reshape.31 = bf16[128,512]{1,0:T(8,128)(2,1)} reshape(bf16[1024,64]{1,0:T(8,128)(2,1)S(1)} %get-tuple-element.47) | data formatting | bytes 262144 | tf_op jit(solution)/shard_map/reshape | solution.py:324
  60.5 1.0 %collective-permute-done.6.got_ref = bf16[16,640]{1,0:T(8,128)(2,1)S(1)} collective-permute-done((bf16[16,640]{1,0:T(8,128)(2,1)S(1)}, bf16[16,640]{1,0:T(8,128)(2,1)S(1)}, u32[]{:S(2)}, u32[]{:S(2)}) %collective-permute-start.6) | collective-permute-done | bytes 20512 | tf_op jit(solution)/shard_map/ppermute | solution.py:349
  61.5 0.6 shard_map.119
  (1 shorter events, 0.0 us)
Async XLA Ops:
  0.6 13.0 %copy-start.2 = (bf16[128,512]{1,0:T(8,128)(2,1)S(1)}, bf16[128,512]{1,0:T(8,128)(2,1)}, u32[]{:S(2)}) copy-start(bf16[128,512]{1,0:T(8,128)(2,1)} %param.9) | copy-start | bytes 393220
  0.6 13.2 %copy-start = (bf16[128,8,512]{2,1,0:T(8,128)(2,1)S(1)}, bf16[128,8,512]{2,1,0:T(8,128)(2,1)}, u32[]{:S(2)}) copy-start(bf16[128,8,512]{2,1,0:T(8,128)(2,1)} %param.8) | copy-start | bytes 3145732
  0.7 13.2 %copy-start.1 = (bf16[128,8,512]{2,1,0:T(8,128)(2,1)S(1)}, bf16[128,8,512]{2,1,0:T(8,128)(2,1)}, u32[]{:S(2)}) copy-start(bf16[128,8,512]{2,1,0:T(8,128)(2,1)} %param.10) | copy-start | bytes 3145732
  1.8 12.0 %collective-permute-start = (bf16[144,512]{1,0:T(8,128)(2,1)S(1)}, bf16[144,512]{1,0:T(8,128)(2,1)S(1)}, u32[]{:S(2)}, u32[]{:S(2)}) collective-permute-start(bf16[144,512]{1,0:T(8,128)(2,1)S(1)} %get-tuple-element.33.own_ref), channel_id=1, source_target_pairs={{0,8},{1,9},{2,10},{3,11},{4,12},{5,13},{6,14},{7,15},{8,32},{9,33... | collective-permute-start | bytes 442376 | tf_op jit(solution)/shard_map/ppermute | solution.py:24
  8.1 15.7 %collective-permute-start.1 = (bf16[144,512]{1,0:T(8,128)(2,1)S(1)}, bf16[144,512]{1,0:T(8,128)(2,1)S(1)}, u32[]{:S(2)}, u32[]{:S(2)}) collective-permute-start(bf16[144,512]{1,0:T(8,128)(2,1)S(1)} %get-tuple-element.33.own_ref), channel_id=1, source_target_pairs={{0,16},{1,17},{2,18},{3,19},{4,20},{5,21},{6,22},{7,23},{8,24},{9,... | collective-permute-start | bytes 442376 | tf_op jit(solution)/shard_map/ppermute | solution.py:24
  11.7 14.7 %collective-permute-start.2 = (bf16[144,512]{1,0:T(8,128)(2,1)S(1)}, bf16[144,512]{1,0:T(8,128)(2,1)S(1)}, u32[]{:S(2)}, u32[]{:S(2)}) collective-permute-start(bf16[144,512]{1,0:T(8,128)(2,1)S(1)} %get-tuple-element.33.own_ref), channel_id=1, source_target_pairs={{0,24},{1,25},{2,26},{3,27},{4,28},{5,29},{6,30},{7,31},{8,16},{9,... | collective-permute-start | bytes 442376 | tf_op jit(solution)/shard_map/ppermute | solution.py:24
  16.0 15.1 %collective-permute-start.3 = (bf16[128,640]{1,0:T(8,128)(2,1)S(1)}, bf16[128,640]{1,0:T(8,128)(2,1)S(1)}, u32[]{:S(2)}, u32[]{:S(2)}) collective-permute-start(bf16[128,640]{1,0:T(8,128)(2,1)S(1)} %get-tuple-element.50), channel_id=1, source_target_pairs={{0,505},{1,504},{2,507},{3,506},{4,509},{5,508},{6,511},{7,510},{8... | collective-permute-start | bytes 491528 | tf_op jit(solution)/shard_map/ppermute | solution.py:24
  28.5 3.6 %collective-permute-start.4 = (bf16[128,640]{1,0:T(8,128)(2,1)S(1)}, bf16[128,640]{1,0:T(8,128)(2,1)S(1)}, u32[]{:S(2)}, u32[]{:S(2)}) collective-permute-start(bf16[128,640]{1,0:T(8,128)(2,1)S(1)} %get-tuple-element.53), channel_id=1, source_target_pairs={{0,8},{1,9},{2,10},{3,11},{4,12},{5,13},{6,14},{7,15},{8,0},{9,1},... | collective-permute-start | bytes 491528 | tf_op jit(solution)/shard_map/ppermute | solution.py:24
  42.7 5.3 %collective-permute-start.5 = (bf16[32,640]{1,0:T(8,128)(2,1)S(1)}, bf16[32,640]{1,0:T(8,128)(2,1)S(1)}, u32[]{:S(2)}, u32[]{:S(2)}) collective-permute-start(bf16[32,640]{1,0:T(8,128)(2,1)S(1)} %get-tuple-element.55), channel_id=1, source_target_pairs={{0,497},{1,496},{2,499},{3,498},{4,501},{5,500},{6,503},{7,502},{8... | collective-permute-start | bytes 122888 | tf_op jit(solution)/shard_map/ppermute | solution.py:24
  48.0 13.4 %collective-permute-start.6 = (bf16[16,640]{1,0:T(8,128)(2,1)S(1)}, bf16[16,640]{1,0:T(8,128)(2,1)S(1)}, u32[]{:S(2)}, u32[]{:S(2)}) collective-permute-start(bf16[16,640]{1,0:T(8,128)(2,1)S(1)} %get-tuple-element.57), channel_id=1, source_target_pairs={{0,1},{1,0},{2,3},{3,2},{4,5},{5,4},{6,7},{7,6},{8,9},{9,8},{10,11... | collective-permute-start | bytes 61448 | tf_op jit(solution)/shard_map/ppermute | solution.py:349

commit v5 on v4

--- a/solution.py
+++ b/solution.py
@@ -75,10 +75,13 @@
     return jnp.minimum(first, second), jnp.maximum(first, second), lower, upper
 
 
-def tile(keys, ropes, key_blocks, row_block, q, qr, do, total, dots):
-    rows = q.shape[0]
-    scores = SOFTMAX_SCALE * (nt(keys, q) + nt(ropes, qr))
-    probs = jnp.exp(scores - total)
+def products(keys, ropes, q, qr, do):
+    return nt(keys, q) + nt(ropes, qr), nt(keys, do)
+
+
+def weigh(scores, dprobs, key_blocks, row_block, total, dots):
+    rows = scores.shape[1]
+    probs = jnp.exp(SOFTMAX_SCALE * scores - total)
     ahead = (
         lax.broadcasted_iota(jnp.int32, (BLK, rows), 1) // (rows // BLK)
         - lax.broadcasted_iota(jnp.int32, (BLK, rows), 0)
@@ -90,20 +93,27 @@
             piece = jnp.where(ahead >= (key_block - row_block) * BLK, piece, 0.0)
         pieces.append(piece)
     probs = jnp.concatenate(pieces, axis=0)
-    dprobs = nt(keys, do)
     dscores = (SOFTMAX_SCALE * probs * (dprobs - dots)).astype(jnp.bfloat16)
     return probs.astype(jnp.bfloat16), dscores
 
 
-def pack_kernel(lat_hbm, rope_hbm, order_hbm, dot_hbm, tot_hbm, own_ref, order_ref, dot_ref, tot_ref, sems):
-    pairs = [(lat_hbm, own_ref.at[pl.ds(0, 128), :])]
-    for b in range(4):
-        pairs.append((rope_hbm.at[pl.ds(16 * b, 16), :], own_ref.at[pl.ds(128, 16), pl.ds(128 * b, 128)]))
-    pairs += [(order_hbm, order_ref), (dot_hbm, dot_ref), (tot_hbm, tot_ref)]
+def pack_kernel(
+    lat_hbm, rope_hbm, order_hbm, dot_hbm, tot_hbm, own_ref, order_ref, dot_ref, tot_ref, rope_ref, sems
+):
+    pairs = (
+        (rope_hbm, rope_ref),
+        (lat_hbm, own_ref.at[pl.ds(0, 128), :]),
+        (dot_hbm, dot_ref),
+        (tot_hbm, tot_ref),
+        (order_hbm, order_ref),
+    )
     copies = [pltpu.make_async_copy(pair[0], pair[1], sems.at[n]) for n, pair in enumerate(pairs)]
     for copy in copies:
         copy.start()
-    for copy in copies:
+    copies[0].wait()
+    for b in range(4):
+        own_ref[128:, 128 * b : 128 * (b + 1)] = rope_ref[16 * b : 16 * (b + 1), :]
+    for copy in copies[1:]:
         copy.wait()
 
 
@@ -132,16 +142,17 @@
     keys_ref[...] = keys
     ropes_ref[...] = ropes
 
-    def grads(part, key_rows, row_block, seen, ds_ref):
-        q, qr, do = q_ref[part, :], qr_ref[part, :], do_ref[part, :]
-        probs, ds = tile(
-            keys[:key_rows], ropes[:key_rows], seen, row_block, q, qr, do, tot_ref[:, part], dot_ref[:, part]
-        )
-        ds_ref[...] = ds
-        return nn(ds, q) + nn(probs, do), nn(ds, qr)
-
-    lat, grope = grads(pl.ds(upper, rows), 4 * BLK, high_mine, [None, None] + blocks[2:], ds_up_ref)
-    lat_low, grope_low = grads(pl.ds(lower, rows), 2 * BLK, low_mine, blocks[:2], ds_low_ref)
+    up, low = pl.ds(upper, rows), pl.ds(lower, rows)
+    s_up, d_up = products(keys, ropes, q_ref[up, :], qr_ref[up, :], do_ref[up, :])
+    s_low, d_low = products(keys[: 2 * BLK], ropes[: 2 * BLK], q_ref[low, :], qr_ref[low, :], do_ref[low, :])
+    p_up, ds_up = weigh(s_up, d_up, [None, None] + blocks[2:], high_mine, tot_ref[:, up], dot_ref[:, up])
+    ds_up_ref[...] = ds_up
+    p_low, ds_low = weigh(s_low, d_low, blocks[:2], low_mine, tot_ref[:, low], dot_ref[:, low])
+    ds_low_ref[...] = ds_low
+    lat = nn(ds_up, q_ref[up, :]) + nn(p_up, do_ref[up, :])
+    grope = nn(ds_up, qr_ref[up, :])
+    lat_low = nn(ds_low, q_ref[low, :]) + nn(p_low, do_ref[low, :])
+    grope_low = nn(ds_low, qr_ref[low, :])
     blank = jnp.zeros((BLK, WIDE - 512 - 64), jnp.float32)
     found = []
     for n in range(4):
@@ -284,7 +295,7 @@
             (forward_dot.shape, f32),
             (log_total.shape, f32),
         ],
-        [pltpu.SemaphoreType.DMA((8,))],
+        [pltpu.VMEM((64, 128), bf16), pltpu.SemaphoreType.DMA((5,))],
         20.0,
     )
     first = permute(own, lambda i: i + 3 if i % 2 else i + 1)

time: 63 us -> 63 us (level)
  no operation moved by 1% of the time
where the time goes in v5:
time: 63 us; the launch traced here: 62.1 us
  starting transfers between devices  35.6 us (57%)
  blocking collectives  10.4 us (17%)
  Pallas kernels  8.61 us (14%)
  waiting for transfers between devices  5.51 us (9%)
  local copies, waits for them, and re-layouts  1.06 us (2%)
  between operations  0.81 us (1%)
    ppermute x6, starting transfers between devices, permute(): return lax.ppermute(value, ('seq', 'head'), pairs)  26.4 us
    all_to_all x1, blocking collectives, shards(): lax.all_to_all(joined, 'head', 0, 0, tiled=True, axis_index_groups=[[0, 2...  10.4 us
    ppermute x1, starting transfers between devices, shards(): got = lax.ppermute(given, 'head', [(h, h ^ 1) for h in range(8)])  9.28 us
    pallas_call x9, Pallas kernels, call(): pl.pallas_call(kernel, out_shape=tuple((jax.ShapeDtypeStruct(shape, dtype...  8.61 us
    ppermute x6, waiting for transfers between devices, permute(): return lax.ppermute(value, ('seq', 'head'), pairs)  4.53 us
  transfers between devices with their start and end apart: 7, of which 4 were waited for; matrix products, arithmetic and copies ran while one was open for 2% of the time, Pallas kernels for 11%

profile of v5, /device:TPU:1, one launch (start us, length us, event | category | flops | bytes accessed | tf_op | source)
XLA Modules:
  0.0 62.1 jit_solution(2925491198111225166)
XLA Ops:
  0.6 0.0 copy-start.2
  0.6 0.0 copy-start
  0.7 0.0 copy-start.1
  0.7 1.1 %shard_map.111 = (bf16[144,512]{1,0:T(8,128)(2,1)S(1)}, s32[128]{0:T(128)S(1)}, f32[8,128]{1,0:T(8,128)S(1)}, f32[8,128]{1,0:T(8,128)S(1)}) custom-call(bf16[128,512]{1,0:T(8,128)(2,1)} %lat_hbm.1, bf16[64,128]{1,0:T(8,128)(2,1)} %rope_hbm.1, s32[128]{0:T(128)} %order_hbm.1, f32[8,128]{1,0:T(8,128)} %dot_hbm.1, f32[8,128]{1,0:T(8,128)} %tot_hbm.1), custom_call_target="tpu_custom_call" | custom-call | flops 20000000000 | bytes 40000000 | tf_op jit(solution)/shard_map/pallas_call | solution.py:230
  1.8 6.3 %collective-permute-start = (bf16[144,512]{1,0:T(8,128)(2,1)S(1)}, bf16[144,512]{1,0:T(8,128)(2,1)S(1)}, u32[]{:S(2)}, u32[]{:S(2)}) collective-permute-start(bf16[144,512]{1,0:T(8,128)(2,1)S(1)} %get-tuple-element.33.own_ref), channel_id=1, source_target_pairs={{0,8},{1,9},{2,10},{3,11},{4,12},{5,13},{6,14},{7,15},{8,32},{9,33... | collective-permute-start | bytes 442376 | tf_op jit(solution)/shard_map/ppermute | solution.py:24
  8.1 3.5 %collective-permute-start.1 = (bf16[144,512]{1,0:T(8,128)(2,1)S(1)}, bf16[144,512]{1,0:T(8,128)(2,1)S(1)}, u32[]{:S(2)}, u32[]{:S(2)}) collective-permute-start(bf16[144,512]{1,0:T(8,128)(2,1)S(1)} %get-tuple-element.33.own_ref), channel_id=1, source_target_pairs={{0,16},{1,17},{2,18},{3,19},{4,20},{5,21},{6,22},{7,23},{8,24},{9,... | collective-permute-start | bytes 442376 | tf_op jit(solution)/shard_map/ppermute | solution.py:24
  11.6 1.9 %collective-permute-start.2 = (bf16[144,512]{1,0:T(8,128)(2,1)S(1)}, bf16[144,512]{1,0:T(8,128)(2,1)S(1)}, u32[]{:S(2)}, u32[]{:S(2)}) collective-permute-start(bf16[144,512]{1,0:T(8,128)(2,1)S(1)} %get-tuple-element.33.own_ref), channel_id=1, source_target_pairs={{0,24},{1,25},{2,26},{3,27},{4,28},{5,29},{6,30},{7,31},{8,16},{9,... | collective-permute-start | bytes 442376 | tf_op jit(solution)/shard_map/ppermute | solution.py:24
  13.6 0.0 copy-done.2
  13.6 0.2 reshape.28.qr_ref
  13.8 0.0 collective-permute-done.near_ref
  13.8 0.0 copy-done
  13.8 0.0 copy-done.1
  13.8 2.2 %shard_map.112 = (f32[128,640]{1,0:T(8,128)S(1)}, bf16[128,640]{1,0:T(8,128)(2,1)S(1)}, bf16[256,512]{1,0:T(8,128)(2,1)S(1)}, bf16[128,512]{1,0:T(8,128)(2,1)S(1...) custom-call(s32[128]{0:T(128)S(1)} %get-tuple-element.32.order_ref, ...), custom_call_target="tpu_custom_call" | custom-call | tf_op jit(solution)/shard_map/pallas_call | solution.py:230
  16.0 7.8 %collective-permute-start.3 = (bf16[128,640]{1,0:T(8,128)(2,1)S(1)}, bf16[128,640]{1,0:T(8,128)(2,1)S(1)}, u32[]{:S(2)}, u32[]{:S(2)}) collective-permute-start(bf16[128,640]{1,0:T(8,128)(2,1)S(1)} %get-tuple-element.50), channel_id=1, source_target_pairs={{0,505},{1,504},{2,507},{3,506},{4,509},{5,508},{6,511},{7,510},{8... | collective-permute-start | bytes 491528 | tf_op jit(solution)/shard_map/ppermute | solution.py:24
  23.8 0.0 collective-permute-done.1.two_ref
  23.8 2.5 %collective-permute-done.2.last_ref = bf16[144,512]{1,0:T(8,128)(2,1)S(1)} collective-permute-done((bf16[144,512]{1,0:T(8,128)(2,1)S(1)}, bf16[144,512]{1,0:T(8,128)(2,1)S(1)}, u32[]{:S(2)}, u32[]{:S(2)}) %collective-permute-start.2) | collective-permute-done | bytes 147488 | tf_op jit(solution)/shard_map/ppermute | solution.py:24
  26.3 2.1 %shard_map.113 = (f32[128,640]{1,0:T(8,128)S(1)}, bf16[128,640]{1,0:T(8,128)(2,1)S(1)}, bf16[256,512]{1,0:T(8,128)(2,1)S(1)}, bf16[128,512]{1,0:T(8,128)(2,1)S(1...) custom-call(s32[128]{0:T(128)S(1)} %get-tuple-element.32.order_ref, ...), custom_call_target="tpu_custom_call" | custom-call | tf_op jit(solution)/shard_map/pallas_call | solution.py:230
  28.4 2.6 %collective-permute-start.4 = (bf16[128,640]{1,0:T(8,128)(2,1)S(1)}, bf16[128,640]{1,0:T(8,128)(2,1)S(1)}, u32[]{:S(2)}, u32[]{:S(2)}) collective-permute-start(bf16[128,640]{1,0:T(8,128)(2,1)S(1)} %get-tuple-element.53), channel_id=1, source_target_pairs={{0,8},{1,9},{2,10},{3,11},{4,12},{5,13},{6,14},{7,15},{8,0},{9,1},... | collective-permute-start | bytes 491528 | tf_op jit(solution)/shard_map/ppermute | solution.py:24
  31.1 0.0 collective-permute-done.3.early_ref
  31.1 0.1 shard_map.115
  31.2 0.9 %collective-permute-done.4.late_ref = bf16[128,640]{1,0:T(8,128)(2,1)S(1)} collective-permute-done((bf16[128,640]{1,0:T(8,128)(2,1)S(1)}, bf16[128,640]{1,0:T(8,128)(2,1)S(1)}, u32[]{:S(2)}, u32[]{:S(2)}) %collective-permute-start.4) | collective-permute-done | bytes 163872 | tf_op jit(solution)/shard_map/ppermute | solution.py:24
  32.1 0.1 shard_map.116
  32.2 10.4 %all_to_all.9.parts_ref = bf16[4,32,1152]{2,1,0:T(8,128)(2,1)S(1)} all-to-all(bf16[4,32,1152]{2,1,0:T(8,128)(2,1)S(1)} %bitcast.8), channel_id=1, replica_groups={{0,2,4,6},{1,3,5,7},{8,10,12,14},{9,11,13,15},{16,18,20,22},{17,19,21,2..., dimensions={0} | all-to-all | bytes 589824 | tf_op jit(solution)/shard_map/all_to_all | solution.py:345
  42.6 0.1 shard_map.117
  42.7 4.2 %collective-permute-start.5 = (bf16[32,640]{1,0:T(8,128)(2,1)S(1)}, bf16[32,640]{1,0:T(8,128)(2,1)S(1)}, u32[]{:S(2)}, u32[]{:S(2)}) collective-permute-start(bf16[32,640]{1,0:T(8,128)(2,1)S(1)} %get-tuple-element.55), channel_id=1, source_target_pairs={{0,497},{1,496},{2,499},{3,498},{4,501},{5,500},{6,503},{7,502},{8... | collective-permute-start | bytes 122888 | tf_op jit(solution)/shard_map/ppermute | solution.py:24
  46.9 1.1 %collective-permute-done.5.got_ref = bf16[32,640]{1,0:T(8,128)(2,1)S(1)} collective-permute-done((bf16[32,640]{1,0:T(8,128)(2,1)S(1)}, bf16[32,640]{1,0:T(8,128)(2,1)S(1)}, u32[]{:S(2)}, u32[]{:S(2)}) %collective-permute-start.5) | collective-permute-done | bytes 40992 | tf_op jit(solution)/shard_map/ppermute | solution.py:24
  48.0 9.3 %collective-permute-start.6 = (bf16[16,640]{1,0:T(8,128)(2,1)S(1)}, bf16[16,640]{1,0:T(8,128)(2,1)S(1)}, u32[]{:S(2)}, u32[]{:S(2)}) collective-permute-start(bf16[16,640]{1,0:T(8,128)(2,1)S(1)} %get-tuple-element.57), channel_id=1, source_target_pairs={{0,1},{1,0},{2,3},{3,2},{4,5},{5,4},{6,7},{7,6},{8,9},{9,8},{10,11... | collective-permute-start | bytes 61448 | tf_op jit(solution)/shard_map/ppermute | solution.py:360
  57.3 2.3 %shard_map.114 = (bf16[1024,512]{1,0:T(8,128)(2,1)}, bf16[1024,64]{1,0:T(8,128)(2,1)S(1)}) custom-call(s32[128]{0:T(128)S(1)} %get-tuple-element.32.order_ref, bf16[256,512]{1,0:T(8,128)(2,1)S(1)} %get-tuple-element.36.up_a_ref, bf16[128,512]{1,0:T(8,128)(2,1)S(1)} %get-tuple-element.37.low_a_ref, bf16[256,512]{1,0:T(8,128)(2,1)S(1)} %get-tuple-element.38.keys_a_ref, ...), custom_call_target="tpu_custom_call" | custom-call | flops 50000000 | bytes 100000 | tf_op jit(solution)/shard_map/pallas_call | solution.py:230
  59.6 0.9 %reshape.31 = bf16[128,512]{1,0:T(8,128)(2,1)} reshape(bf16[1024,64]{1,0:T(8,128)(2,1)S(1)} %get-tuple-element.47) | data formatting | bytes 262144 | tf_op jit(solution)/shard_map/reshape | solution.py:335
  60.5 1.0 %collective-permute-done.6.got_ref = bf16[16,640]{1,0:T(8,128)(2,1)S(1)} collective-permute-done((bf16[16,640]{1,0:T(8,128)(2,1)S(1)}, bf16[16,640]{1,0:T(8,128)(2,1)S(1)}, u32[]{:S(2)}, u32[]{:S(2)}) %collective-permute-start.6) | collective-permute-done | bytes 20512 | tf_op jit(solution)/shard_map/ppermute | solution.py:360
  61.4 0.6 shard_map.119
  (1 shorter events, 0.0 us)
Async XLA Ops:
  0.6 12.9 %copy-start.2 = (bf16[128,512]{1,0:T(8,128)(2,1)S(1)}, bf16[128,512]{1,0:T(8,128)(2,1)}, u32[]{:S(2)}) copy-start(bf16[128,512]{1,0:T(8,128)(2,1)} %param.9) | copy-start | bytes 393220
  0.6 13.1 %copy-start = (bf16[128,8,512]{2,1,0:T(8,128)(2,1)S(1)}, bf16[128,8,512]{2,1,0:T(8,128)(2,1)}, u32[]{:S(2)}) copy-start(bf16[128,8,512]{2,1,0:T(8,128)(2,1)} %param.8) | copy-start | bytes 3145732
  0.7 13.1 %copy-start.1 = (bf16[128,8,512]{2,1,0:T(8,128)(2,1)S(1)}, bf16[128,8,512]{2,1,0:T(8,128)(2,1)}, u32[]{:S(2)}) copy-start(bf16[128,8,512]{2,1,0:T(8,128)(2,1)} %param.10) | copy-start | bytes 3145732
  1.8 12.0 %collective-permute-start = (bf16[144,512]{1,0:T(8,128)(2,1)S(1)}, bf16[144,512]{1,0:T(8,128)(2,1)S(1)}, u32[]{:S(2)}, u32[]{:S(2)}) collective-permute-start(bf16[144,512]{1,0:T(8,128)(2,1)S(1)} %get-tuple-element.33.own_ref), channel_id=1, source_target_pairs={{0,8},{1,9},{2,10},{3,11},{4,12},{5,13},{6,14},{7,15},{8,32},{9,33... | collective-permute-start | bytes 442376 | tf_op jit(solution)/shard_map/ppermute | solution.py:24
  8.1 15.7 %collective-permute-start.1 = (bf16[144,512]{1,0:T(8,128)(2,1)S(1)}, bf16[144,512]{1,0:T(8,128)(2,1)S(1)}, u32[]{:S(2)}, u32[]{:S(2)}) collective-permute-start(bf16[144,512]{1,0:T(8,128)(2,1)S(1)} %get-tuple-element.33.own_ref), channel_id=1, source_target_pairs={{0,16},{1,17},{2,18},{3,19},{4,20},{5,21},{6,22},{7,23},{8,24},{9,... | collective-permute-start | bytes 442376 | tf_op jit(solution)/shard_map/ppermute | solution.py:24
  11.6 14.7 %collective-permute-start.2 = (bf16[144,512]{1,0:T(8,128)(2,1)S(1)}, bf16[144,512]{1,0:T(8,128)(2,1)S(1)}, u32[]{:S(2)}, u32[]{:S(2)}) collective-permute-start(bf16[144,512]{1,0:T(8,128)(2,1)S(1)} %get-tuple-element.33.own_ref), channel_id=1, source_target_pairs={{0,24},{1,25},{2,26},{3,27},{4,28},{5,29},{6,30},{7,31},{8,16},{9,... | collective-permute-start | bytes 442376 | tf_op jit(solution)/shard_map/ppermute | solution.py:24
  16.0 15.1 %collective-permute-start.3 = (bf16[128,640]{1,0:T(8,128)(2,1)S(1)}, bf16[128,640]{1,0:T(8,128)(2,1)S(1)}, u32[]{:S(2)}, u32[]{:S(2)}) collective-permute-start(bf16[128,640]{1,0:T(8,128)(2,1)S(1)} %get-tuple-element.50), channel_id=1, source_target_pairs={{0,505},{1,504},{2,507},{3,506},{4,509},{5,508},{6,511},{7,510},{8... | collective-permute-start | bytes 491528 | tf_op jit(solution)/shard_map/ppermute | solution.py:24
  28.4 3.6 %collective-permute-start.4 = (bf16[128,640]{1,0:T(8,128)(2,1)S(1)}, bf16[128,640]{1,0:T(8,128)(2,1)S(1)}, u32[]{:S(2)}, u32[]{:S(2)}) collective-permute-start(bf16[128,640]{1,0:T(8,128)(2,1)S(1)} %get-tuple-element.53), channel_id=1, source_target_pairs={{0,8},{1,9},{2,10},{3,11},{4,12},{5,13},{6,14},{7,15},{8,0},{9,1},... | collective-permute-start | bytes 491528 | tf_op jit(solution)/shard_map/ppermute | solution.py:24
  42.7 5.3 %collective-permute-start.5 = (bf16[32,640]{1,0:T(8,128)(2,1)S(1)}, bf16[32,640]{1,0:T(8,128)(2,1)S(1)}, u32[]{:S(2)}, u32[]{:S(2)}) collective-permute-start(bf16[32,640]{1,0:T(8,128)(2,1)S(1)} %get-tuple-element.55), channel_id=1, source_target_pairs={{0,497},{1,496},{2,499},{3,498},{4,501},{5,500},{6,503},{7,502},{8... | collective-permute-start | bytes 122888 | tf_op jit(solution)/shard_map/ppermute | solution.py:24
  48.0 13.5 %collective-permute-start.6 = (bf16[16,640]{1,0:T(8,128)(2,1)S(1)}, bf16[16,640]{1,0:T(8,128)(2,1)S(1)}, u32[]{:S(2)}, u32[]{:S(2)}) collective-permute-start(bf16[16,640]{1,0:T(8,128)(2,1)S(1)} %get-tuple-element.57), channel_id=1, source_target_pairs={{0,1},{1,0},{2,3},{3,2},{4,5},{5,4},{6,7},{7,6},{8,9},{9,8},{10,11... | collective-permute-start | bytes 61448 | tf_op jit(solution)/shard_map/ppermute | solution.py:360

commit v6 on v4

--- a/solution.py
+++ b/solution.py
@@ -77,8 +77,8 @@
 
 def tile(keys, ropes, key_blocks, row_block, q, qr, do, total, dots):
     rows = q.shape[0]
-    scores = SOFTMAX_SCALE * (nt(keys, q) + nt(ropes, qr))
-    probs = jnp.exp(scores - total)
+    scores = nt(keys, q) + nt(ropes, qr)
+    probs = jnp.exp(SOFTMAX_SCALE * scores - total)
     ahead = (
         lax.broadcasted_iota(jnp.int32, (BLK, rows), 1) // (rows // BLK)
         - lax.broadcasted_iota(jnp.int32, (BLK, rows), 0)
@@ -91,7 +91,7 @@
         pieces.append(piece)
     probs = jnp.concatenate(pieces, axis=0)
     dprobs = nt(keys, do)
-    dscores = (SOFTMAX_SCALE * probs * (dprobs - dots)).astype(jnp.bfloat16)
+    dscores = (probs * (SOFTMAX_SCALE * dprobs - dots)).astype(jnp.bfloat16)
     return probs.astype(jnp.bfloat16), dscores
 
 
@@ -159,7 +159,7 @@
     rope_ref,
 ):
     me = lax.axis_index("seq")
-    dot_ref[...] = spread(dot_in[...])
+    dot_ref[...] = SOFTMAX_SCALE * spread(dot_in[...])
     tot_ref[...] = spread(tot_in[...])
     shards = (0, jnp.where(lax.rem(me, 2) == 0, 3, 1))
     found = window_part(

time: 63 us -> 63.1 us (level)
  no operation moved by 1% of the time
where the time goes in v6:
time: 63.1 us; the launch traced here: 62.1 us
  starting transfers between devices  35.6 us (56%)
  blocking collectives  10.4 us (16%)
  Pallas kernels  8.7 us (14%)
  waiting for transfers between devices  5.47 us (9%)
  local copies, waits for them, and re-layouts  1.06 us (2%)
  between operations  0.81 us (1%)
    ppermute x6, starting transfers between devices, permute(): return lax.ppermute(value, ('seq', 'head'), pairs)  26.4 us
    all_to_all x1, blocking collectives, shards(): lax.all_to_all(joined, 'head', 0, 0, tiled=True, axis_index_groups=[[0, 2...  10.4 us
    ppermute x1, starting transfers between devices, shards(): got = lax.ppermute(given, 'head', [(h, h ^ 1) for h in range(8)])  9.25 us
    pallas_call x9, Pallas kernels, call(): pl.pallas_call(kernel, out_shape=tuple((jax.ShapeDtypeStruct(shape, dtype...  8.7 us
    ppermute x6, waiting for transfers between devices, permute(): return lax.ppermute(value, ('seq', 'head'), pairs)  4.5 us
  transfers between devices with their start and end apart: 7, of which 4 were waited for; matrix products, arithmetic and copies ran while one was open for 2% of the time, Pallas kernels for 11%

profile of v6, /device:TPU:1, one launch (start us, length us, event | category | flops | bytes accessed | tf_op | source)
XLA Modules:
  0.0 62.1 jit_solution(4482033131740810028)
XLA Ops:
  0.6 0.0 copy-start.2
  0.6 0.0 copy-start
  0.7 0.0 copy-start.1
  0.7 1.1 %shard_map.111 = (bf16[144,512]{1,0:T(8,128)(2,1)S(1)}, s32[128]{0:T(128)S(1)}, f32[8,128]{1,0:T(8,128)S(1)}, f32[8,128]{1,0:T(8,128)S(1)}) custom-call(bf16[128,512]{1,0:T(8,128)(2,1)} %lat_hbm.1, bf16[64,128]{1,0:T(8,128)(2,1)} %rope_hbm.1, s32[128]{0:T(128)} %order_hbm.1, f32[8,128]{1,0:T(8,128)} %dot_hbm.1, f32[8,128]{1,0:T(8,128)} %tot_hbm.1), custom_call_target="tpu_custom_call" | custom-call | flops 20000000000 | bytes 40000000 | tf_op jit(solution)/shard_map/pallas_call | solution.py:219
  1.8 6.3 %collective-permute-start = (bf16[144,512]{1,0:T(8,128)(2,1)S(1)}, bf16[144,512]{1,0:T(8,128)(2,1)S(1)}, u32[]{:S(2)}, u32[]{:S(2)}) collective-permute-start(bf16[144,512]{1,0:T(8,128)(2,1)S(1)} %get-tuple-element.33.own_ref), channel_id=1, source_target_pairs={{0,8},{1,9},{2,10},{3,11},{4,12},{5,13},{6,14},{7,15},{8,32},{9,33... | collective-permute-start | bytes 442376 | tf_op jit(solution)/shard_map/ppermute | solution.py:24
  8.1 3.5 %collective-permute-start.1 = (bf16[144,512]{1,0:T(8,128)(2,1)S(1)}, bf16[144,512]{1,0:T(8,128)(2,1)S(1)}, u32[]{:S(2)}, u32[]{:S(2)}) collective-permute-start(bf16[144,512]{1,0:T(8,128)(2,1)S(1)} %get-tuple-element.33.own_ref), channel_id=1, source_target_pairs={{0,16},{1,17},{2,18},{3,19},{4,20},{5,21},{6,22},{7,23},{8,24},{9,... | collective-permute-start | bytes 442376 | tf_op jit(solution)/shard_map/ppermute | solution.py:24
  11.7 1.9 %collective-permute-start.2 = (bf16[144,512]{1,0:T(8,128)(2,1)S(1)}, bf16[144,512]{1,0:T(8,128)(2,1)S(1)}, u32[]{:S(2)}, u32[]{:S(2)}) collective-permute-start(bf16[144,512]{1,0:T(8,128)(2,1)S(1)} %get-tuple-element.33.own_ref), channel_id=1, source_target_pairs={{0,24},{1,25},{2,26},{3,27},{4,28},{5,29},{6,30},{7,31},{8,16},{9,... | collective-permute-start | bytes 442376 | tf_op jit(solution)/shard_map/ppermute | solution.py:24
  13.6 0.0 copy-done.2
  13.6 0.2 reshape.28.qr_ref
  13.8 0.0 collective-permute-done.near_ref
  13.8 0.0 copy-done
  13.8 0.0 copy-done.1
  13.8 2.2 %shard_map.112 = (f32[128,640]{1,0:T(8,128)S(1)}, bf16[128,640]{1,0:T(8,128)(2,1)S(1)}, bf16[256,512]{1,0:T(8,128)(2,1)S(1)}, bf16[128,512]{1,0:T(8,128)(2,1)S(1...) custom-call(s32[128]{0:T(128)S(1)} %get-tuple-element.32.order_ref, ...), custom_call_target="tpu_custom_call" | custom-call | tf_op jit(solution)/shard_map/pallas_call | solution.py:219
  16.0 7.8 %collective-permute-start.3 = (bf16[128,640]{1,0:T(8,128)(2,1)S(1)}, bf16[128,640]{1,0:T(8,128)(2,1)S(1)}, u32[]{:S(2)}, u32[]{:S(2)}) collective-permute-start(bf16[128,640]{1,0:T(8,128)(2,1)S(1)} %get-tuple-element.50), channel_id=1, source_target_pairs={{0,505},{1,504},{2,507},{3,506},{4,509},{5,508},{6,511},{7,510},{8... | collective-permute-start | bytes 491528 | tf_op jit(solution)/shard_map/ppermute | solution.py:24
  23.8 0.0 collective-permute-done.1.two_ref
  23.9 2.5 %collective-permute-done.2.last_ref = bf16[144,512]{1,0:T(8,128)(2,1)S(1)} collective-permute-done((bf16[144,512]{1,0:T(8,128)(2,1)S(1)}, bf16[144,512]{1,0:T(8,128)(2,1)S(1)}, u32[]{:S(2)}, u32[]{:S(2)}) %collective-permute-start.2) | collective-permute-done | bytes 147488 | tf_op jit(solution)/shard_map/ppermute | solution.py:24
  26.4 2.1 %shard_map.113 = (f32[128,640]{1,0:T(8,128)S(1)}, bf16[128,640]{1,0:T(8,128)(2,1)S(1)}, bf16[256,512]{1,0:T(8,128)(2,1)S(1)}, bf16[128,512]{1,0:T(8,128)(2,1)S(1...) custom-call(s32[128]{0:T(128)S(1)} %get-tuple-element.32.order_ref, ...), custom_call_target="tpu_custom_call" | custom-call | tf_op jit(solution)/shard_map/pallas_call | solution.py:219
  28.5 2.6 %collective-permute-start.4 = (bf16[128,640]{1,0:T(8,128)(2,1)S(1)}, bf16[128,640]{1,0:T(8,128)(2,1)S(1)}, u32[]{:S(2)}, u32[]{:S(2)}) collective-permute-start(bf16[128,640]{1,0:T(8,128)(2,1)S(1)} %get-tuple-element.53), channel_id=1, source_target_pairs={{0,8},{1,9},{2,10},{3,11},{4,12},{5,13},{6,14},{7,15},{8,0},{9,1},... | collective-permute-start | bytes 491528 | tf_op jit(solution)/shard_map/ppermute | solution.py:24
  31.1 0.0 collective-permute-done.3.early_ref
  31.1 0.1 shard_map.115
  31.2 0.9 %collective-permute-done.4.late_ref = bf16[128,640]{1,0:T(8,128)(2,1)S(1)} collective-permute-done((bf16[128,640]{1,0:T(8,128)(2,1)S(1)}, bf16[128,640]{1,0:T(8,128)(2,1)S(1)}, u32[]{:S(2)}, u32[]{:S(2)}) %collective-permute-start.4) | collective-permute-done | bytes 163872 | tf_op jit(solution)/shard_map/ppermute | solution.py:24
  32.1 0.1 shard_map.116
  32.2 10.4 %all_to_all.9.parts_ref = bf16[4,32,1152]{2,1,0:T(8,128)(2,1)S(1)} all-to-all(bf16[4,32,1152]{2,1,0:T(8,128)(2,1)S(1)} %bitcast.8), channel_id=1, replica_groups={{0,2,4,6},{1,3,5,7},{8,10,12,14},{9,11,13,15},{16,18,20,22},{17,19,21,2..., dimensions={0} | all-to-all | bytes 589824 | tf_op jit(solution)/shard_map/all_to_all | solution.py:334
  42.7 0.1 shard_map.117
  42.8 4.2 %collective-permute-start.5 = (bf16[32,640]{1,0:T(8,128)(2,1)S(1)}, bf16[32,640]{1,0:T(8,128)(2,1)S(1)}, u32[]{:S(2)}, u32[]{:S(2)}) collective-permute-start(bf16[32,640]{1,0:T(8,128)(2,1)S(1)} %get-tuple-element.55), channel_id=1, source_target_pairs={{0,497},{1,496},{2,499},{3,498},{4,501},{5,500},{6,503},{7,502},{8... | collective-permute-start | bytes 122888 | tf_op jit(solution)/shard_map/ppermute | solution.py:24
  47.0 1.1 %collective-permute-done.5.got_ref = bf16[32,640]{1,0:T(8,128)(2,1)S(1)} collective-permute-done((bf16[32,640]{1,0:T(8,128)(2,1)S(1)}, bf16[32,640]{1,0:T(8,128)(2,1)S(1)}, u32[]{:S(2)}, u32[]{:S(2)}) %collective-permute-start.5) | collective-permute-done | bytes 40992 | tf_op jit(solution)/shard_map/ppermute | solution.py:24
  48.1 9.3 %collective-permute-start.6 = (bf16[16,640]{1,0:T(8,128)(2,1)S(1)}, bf16[16,640]{1,0:T(8,128)(2,1)S(1)}, u32[]{:S(2)}, u32[]{:S(2)}) collective-permute-start(bf16[16,640]{1,0:T(8,128)(2,1)S(1)} %get-tuple-element.57), channel_id=1, source_target_pairs={{0,1},{1,0},{2,3},{3,2},{4,5},{5,4},{6,7},{7,6},{8,9},{9,8},{10,11... | collective-permute-start | bytes 61448 | tf_op jit(solution)/shard_map/ppermute | solution.py:349
  57.3 2.3 %shard_map.114 = (bf16[1024,512]{1,0:T(8,128)(2,1)}, bf16[1024,64]{1,0:T(8,128)(2,1)S(1)}) custom-call(s32[128]{0:T(128)S(1)} %get-tuple-element.32.order_ref, bf16[256,512]{1,0:T(8,128)(2,1)S(1)} %get-tuple-element.36.up_a_ref, bf16[128,512]{1,0:T(8,128)(2,1)S(1)} %get-tuple-element.37.low_a_ref, bf16[256,512]{1,0:T(8,128)(2,1)S(1)} %get-tuple-element.38.keys_a_ref, ...), custom_call_target="tpu_custom_call" | custom-call | flops 50000000 | bytes 100000 | tf_op jit(solution)/shard_map/pallas_call | solution.py:219
  59.7 0.9 %reshape.31 = bf16[128,512]{1,0:T(8,128)(2,1)} reshape(bf16[1024,64]{1,0:T(8,128)(2,1)S(1)} %get-tuple-element.47) | data formatting | bytes 262144 | tf_op jit(solution)/shard_map/reshape | solution.py:324
  60.5 1.0 %collective-permute-done.6.got_ref = bf16[16,640]{1,0:T(8,128)(2,1)S(1)} collective-permute-done((bf16[16,640]{1,0:T(8,128)(2,1)S(1)}, bf16[16,640]{1,0:T(8,128)(2,1)S(1)}, u32[]{:S(2)}, u32[]{:S(2)}) %collective-permute-start.6) | collective-permute-done | bytes 20512 | tf_op jit(solution)/shard_map/ppermute | solution.py:349
  61.5 0.6 shard_map.119
  (1 shorter events, 0.0 us)
Async XLA Ops:
  0.6 13.0 %copy-start.2 = (bf16[128,512]{1,0:T(8,128)(2,1)S(1)}, bf16[128,512]{1,0:T(8,128)(2,1)}, u32[]{:S(2)}) copy-start(bf16[128,512]{1,0:T(8,128)(2,1)} %param.9) | copy-start | bytes 393220
  0.6 13.2 %copy-start = (bf16[128,8,512]{2,1,0:T(8,128)(2,1)S(1)}, bf16[128,8,512]{2,1,0:T(8,128)(2,1)}, u32[]{:S(2)}) copy-start(bf16[128,8,512]{2,1,0:T(8,128)(2,1)} %param.8) | copy-start | bytes 3145732
  0.7 13.2 %copy-start.1 = (bf16[128,8,512]{2,1,0:T(8,128)(2,1)S(1)}, bf16[128,8,512]{2,1,0:T(8,128)(2,1)}, u32[]{:S(2)}) copy-start(bf16[128,8,512]{2,1,0:T(8,128)(2,1)} %param.10) | copy-start | bytes 3145732
  1.8 12.0 %collective-permute-start = (bf16[144,512]{1,0:T(8,128)(2,1)S(1)}, bf16[144,512]{1,0:T(8,128)(2,1)S(1)}, u32[]{:S(2)}, u32[]{:S(2)}) collective-permute-start(bf16[144,512]{1,0:T(8,128)(2,1)S(1)} %get-tuple-element.33.own_ref), channel_id=1, source_target_pairs={{0,8},{1,9},{2,10},{3,11},{4,12},{5,13},{6,14},{7,15},{8,32},{9,33... | collective-permute-start | bytes 442376 | tf_op jit(solution)/shard_map/ppermute | solution.py:24
  8.1 15.7 %collective-permute-start.1 = (bf16[144,512]{1,0:T(8,128)(2,1)S(1)}, bf16[144,512]{1,0:T(8,128)(2,1)S(1)}, u32[]{:S(2)}, u32[]{:S(2)}) collective-permute-start(bf16[144,512]{1,0:T(8,128)(2,1)S(1)} %get-tuple-element.33.own_ref), channel_id=1, source_target_pairs={{0,16},{1,17},{2,18},{3,19},{4,20},{5,21},{6,22},{7,23},{8,24},{9,... | collective-permute-start | bytes 442376 | tf_op jit(solution)/shard_map/ppermute | solution.py:24
  11.7 14.7 %collective-permute-start.2 = (bf16[144,512]{1,0:T(8,128)(2,1)S(1)}, bf16[144,512]{1,0:T(8,128)(2,1)S(1)}, u32[]{:S(2)}, u32[]{:S(2)}) collective-permute-start(bf16[144,512]{1,0:T(8,128)(2,1)S(1)} %get-tuple-element.33.own_ref), channel_id=1, source_target_pairs={{0,24},{1,25},{2,26},{3,27},{4,28},{5,29},{6,30},{7,31},{8,16},{9,... | collective-permute-start | bytes 442376 | tf_op jit(solution)/shard_map/ppermute | solution.py:24
  16.0 15.1 %collective-permute-start.3 = (bf16[128,640]{1,0:T(8,128)(2,1)S(1)}, bf16[128,640]{1,0:T(8,128)(2,1)S(1)}, u32[]{:S(2)}, u32[]{:S(2)}) collective-permute-start(bf16[128,640]{1,0:T(8,128)(2,1)S(1)} %get-tuple-element.50), channel_id=1, source_target_pairs={{0,505},{1,504},{2,507},{3,506},{4,509},{5,508},{6,511},{7,510},{8... | collective-permute-start | bytes 491528 | tf_op jit(solution)/shard_map/ppermute | solution.py:24
  28.5 3.6 %collective-permute-start.4 = (bf16[128,640]{1,0:T(8,128)(2,1)S(1)}, bf16[128,640]{1,0:T(8,128)(2,1)S(1)}, u32[]{:S(2)}, u32[]{:S(2)}) collective-permute-start(bf16[128,640]{1,0:T(8,128)(2,1)S(1)} %get-tuple-element.53), channel_id=1, source_target_pairs={{0,8},{1,9},{2,10},{3,11},{4,12},{5,13},{6,14},{7,15},{8,0},{9,1},... | collective-permute-start | bytes 491528 | tf_op jit(solution)/shard_map/ppermute | solution.py:24
  42.8 5.3 %collective-permute-start.5 = (bf16[32,640]{1,0:T(8,128)(2,1)S(1)}, bf16[32,640]{1,0:T(8,128)(2,1)S(1)}, u32[]{:S(2)}, u32[]{:S(2)}) collective-permute-start(bf16[32,640]{1,0:T(8,128)(2,1)S(1)} %get-tuple-element.55), channel_id=1, source_target_pairs={{0,497},{1,496},{2,499},{3,498},{4,501},{5,500},{6,503},{7,502},{8... | collective-permute-start | bytes 122888 | tf_op jit(solution)/shard_map/ppermute | solution.py:24
  48.1 13.4 %collective-permute-start.6 = (bf16[16,640]{1,0:T(8,128)(2,1)S(1)}, bf16[16,640]{1,0:T(8,128)(2,1)S(1)}, u32[]{:S(2)}, u32[]{:S(2)}) collective-permute-start(bf16[16,640]{1,0:T(8,128)(2,1)S(1)} %get-tuple-element.57), channel_id=1, source_target_pairs={{0,1},{1,0},{2,3},{3,2},{4,5},{5,4},{6,7},{7,6},{8,9},{9,8},{10,11... | collective-permute-start | bytes 61448 | tf_op jit(solution)/shard_map/ppermute | solution.py:349
